TPU v7x, 256 devices: a whole 4x4x8 slice. The times are simulated.
256 devices in a mesh: row: 2 (over core), col: 8 (over z), depth: 16 (over y, x).
Axes of the slice: x: 4, y: 4, z: 8, core: 2. Of those that a mesh axis runs over, the one named last changes fastest.
Arguments:
- amplitudes: bfloat16 [128, 256], P(('row', 'col'), 'depth'), may hold values from -6 to 6
- integrals: bfloat16 [1200, 307200], P('col', ('row', 'depth')), may hold values from -1 to 1
- virt_irrep: int32 [1200], replicated, may hold values from 0 to 7
- pair_irrep: int32 [128], replicated, may hold values from 0 to 7
- panel_c: int32 [256], P('depth'), may hold values from 0 to 1199
- panel_d: int32 [256], P('depth'), may hold values from 0 to 1199
Outputs:
- ladder: float32 [1200, 153600], P('col', ('row', 'depth'))
All inputs are finite; a program needn't handle non-finite values.
Results may differ from a plain program's by a relative error of at most 0.0003.
Values may be sent and summed in bfloat16 or wider, within the bound.
No kernel may reach another device: no remote copies, remote signals or barrier semaphores. Data moves between devices by JAX's collectives and lax.ppermute only.
A program may use at most 192 MiB of HBM per device.

v0:
```python
import jax
import jax.numpy as jnp
from jax import lax
from jax.sharding import PartitionSpec as P

NV = 1200


def body(amplitudes, integrals, virt_irrep, pair_irrep, panel_c, panel_d):
    gathered = lax.all_gather(amplitudes, ("row", "col"), axis=0, tiled=True)
    pair_sym = jnp.bitwise_xor(virt_irrep[panel_c], virt_irrep[panel_d])
    keep = pair_irrep[:, None] == pair_sym[None, :]
    allowed = jnp.where(keep, gathered, jnp.zeros_like(gathered))
    layers = lax.axis_size("depth")
    a_rows = NV // lax.axis_size("row")
    b_cols = integrals.shape[0]
    own_rows = allowed.shape[0] // layers
    mine = lax.all_to_all(allowed, "depth", split_axis=0, concat_axis=1, tiled=True)
    piece = lax.all_gather(integrals, "depth", axis=1, tiled=True)
    width = piece.shape[1] // a_rows
    shaped = piece.reshape(b_cols, width, a_rows)
    full = jnp.einsum("jc,bca->jba", mine, shaped, preferred_element_type=jnp.float32)
    a_start = lax.axis_index("row") * a_rows
    b_start = lax.axis_index("col") * b_cols
    ij_start = lax.axis_index("depth") * own_rows
    irrep_a = lax.dynamic_slice_in_dim(virt_irrep, a_start, a_rows, 0)
    irrep_b = lax.dynamic_slice_in_dim(virt_irrep, b_start, b_cols, 0)
    irrep_ij = lax.dynamic_slice_in_dim(pair_irrep, ij_start, own_rows, 0)
    ab_sym = jnp.bitwise_xor(irrep_b[:, None], irrep_a[None, :])
    mask = irrep_ij[:, None, None] == ab_sym[None, :, :]
    masked = jnp.where(mask, full, jnp.float32(0.0))
    return jnp.transpose(masked, (1, 0, 2)).reshape(b_cols, own_rows * a_rows)


def solution(mesh):
    return jax.shard_map(
        body,
        mesh=mesh,
        in_specs=(
            P(("row", "col"), "depth"),
            P("col", ("row", "depth")),
            P(),
            P(),
            P("depth"),
            P("depth"),
        ),
        out_specs=P("col", ("row", "depth")),
        check_vma=False,
    )
```

profile of v0, /device:TPU:2, one launch (start us, length us, event | category | flops | bytes accessed | tf_op | source)
XLA Modules:
  0.0 419.9 jit_solution(5423290619542079237)
XLA Ops:
  6.5 0.0 copy-start
  6.5 0.0 copy-start.3
  6.5 0.0 copy-start.1
  6.5 0.0 copy-start.2
  6.5 0.0 all-gather.2.cloned.1.call-start
  6.6 0.7 all-gather.2.cloned.1.call-update
  7.3 0.7 compare_select_fusion.2
  7.9 0.0 copy-done
  7.9 0.7 gather_fusion
  8.6 0.0 copy-done.3
  8.6 0.7 gather_fusion.1
  9.3 0.0 copy-done.1
  9.3 29.0 %all_gather.6 = bf16[128,16]{1,0:T(8,128)(2,1)S(1)} all-gather(bf16[8,16]{1,0:T(8,128)(2,1)S(1)} %copy-done.1), channel_id=1, replica_groups=mesh['row'=2,'col'=8,'depth'=16] {'row','col'}, dimensions={0}, use_global_device_ids=true | all-gather | bytes 4352 | tf_op jit(solution)/shard_map/all_gather | solution.py:10
  38.3 0.0 copy-done.2
  38.3 0.7 fusion
  39.0 7.3 %all-to-all-start = ((bf16[16,8,16]{2,1,0:T(8,128)(2,1)}), bf16[16,8,16]{2,1,0:T(8,128)(2,1)S(1)}, u32[]{:S(2)}, u32[]{:S(2)}) async-start(bf16[16,8,16]{2,1,0:T(8,128)(2,1)} %fusion), calls=%async_computation | async-start | bytes 65536 | tf_op jit(solution)/shard_map/all_to_all | solution.py:18
  46.3 0.1 dynamic_slice.11
  46.4 0.1 dynamic_slice.10
  46.5 0.1 broadcast_xor_fusion
  46.6 0.1 dynamic_slice.9
  46.7 6.1 %all-to-all-done = bf16[16,8,16]{2,1,0:T(8,128)(2,1)S(1)} async-done(((bf16[16,8,16]{2,1,0:T(8,128)(2,1)}), bf16[16,8,16]{2,1,0:T(8,128)(2,1)S(1)}, u32[]{:S(2)}, u32[]{:S(2)}) %all-to-all-start) | async-done | bytes 4128 | tf_op jit(solution)/shard_map/all_to_all | solution.py:18
  52.8 0.1 reshape.63
  52.9 229.6 %all-gather.2.cloned.1.call-done = bf16[150,153600]{1,0:T(8,128)(2,1)} async-done(((bf16[150,9600]{1,0:T(8,128)(2,1)}), bf16[150,153600]{1,0:T(8,128)(2,1)}) %all-gather.2.cloned.1.call-update) | async-done | bytes 46080016 | tf_op jit(solution)/shard_map/all_gather | solution.py:19
  282.5 108.9 %reshape.43 = bf16[150,256,600]{2,1,0:T(8,128)(2,1)} reshape(bf16[150,153600]{1,0:T(8,128)(2,1)} %all-gather.2.cloned.1.call-done) | data formatting | bytes 92160000 | tf_op jit(solution)/shard_map/reshape | solution.py:21
  391.3 18.5 %bitcast_select_fusion = f32[150,8,600]{2,1,0:T(8,128)S(1)} fusion(bf16[8,256,1]{1,0,2:T(8,128)(2,1)S(1)} %reshape.63, bf16[150,256,600]{2,1,0:T(8,128)(2,1)} %reshape.43, s32[150,600]{1,0:T(8,128)S(1)} %broadcast_xor_fusion, s32[8]{0:T(128)S(1)} %dynamic_slice.9), kind=kOutput, calls=%fused_computation.2 | convolution fusion | flops 370080000 | bytes 49324128 | tf_op jit(solution)/shard_map/jc,bca->jba/dot_general | solution.py:22
  409.8 3.3 reshape.44
  (5 shorter events, 0.0 us)
Async XLA Ops:
  6.5 1.4 copy-start
  6.5 2.1 copy-start.3
  6.5 2.7 copy-start.1
  6.5 31.8 %copy-start.2 = (s32[128]{0:T(128)S(1)}, s32[128]{0:T(128)}, u32[]{:S(2)}) copy-start(s32[128]{0:T(128)} %param.9) | copy-start | bytes 1540
  6.5 275.9 %all-gather.2.cloned.1.call-start = ((), (), s32[]{:S(2)}) async-start(), calls=%async_computation.1 | async-start | bytes 49612800 | tf_op jit(solution)/shard_map/all_gather | solution.py:19
  39.0 13.7 %all-to-all-start = ((bf16[16,8,16]{2,1,0:T(8,128)(2,1)}), bf16[16,8,16]{2,1,0:T(8,128)(2,1)S(1)}, u32[]{:S(2)}, u32[]{:S(2)}) async-start(bf16[16,8,16]{2,1,0:T(8,128)(2,1)} %fusion), calls=%async_computation | async-start | bytes 65536 | tf_op jit(solution)/shard_map/all_to_all | solution.py:18
Sparse Core Ops, SparseCore 0:
  9.9 272.5 all-gather.1
where the time goes:
time: 421 us; the launch traced here: 420 us
  waiting for transfers between devices  236 us (56%)
  local copies, waits for them, and re-layouts  114 us (27%)
  blocking collectives  29 us (7%)
  matrix products  18.5 us (4%)
  between operations  13.4 us (3%)
  starting transfers between devices  7.33 us (2%)
    all_gather x1, waiting for transfers between devices, body(): piece = lax.all_gather(integrals, 'depth', axis=1, tiled=True)  230 us
    reshape x1, local copies, waits for them, and re-layouts, body(): shaped = piece.reshape(b_cols, width, a_rows)  109 us
    all_gather x1, blocking collectives, body(): gathered = lax.all_gather(amplitudes, ('row', 'col'), axis=0, tiled=True)  29 us
    dot_general x1, matrix products, body(): jnp.einsum('jc,bca->jba', mine, shaped, preferred_element_type=jnp.float32)  18.5 us
  transfers between devices with their start and end apart: 2, of which 2 were waited for; matrix products, arithmetic and copies ran while one was open for 1% of the time, Pallas kernels for 0%

commit v1 on v0

v1 whole, which is shorter than its diff:
```python
import jax
import jax.numpy as jnp
from jax import lax
from jax.experimental import pallas as pl
from jax.experimental.pallas import tpu as pltpu
from jax.sharding import PartitionSpec as P

NV = 1200
LAYERS = 16
A_ROWS = 600
B_COLS = 150
A_PAD = 640
B_PAD = 160
CDS = 16
OWN_IJ = 8
CAP_IN = 40
CAP_OUT = 24
PER = 10
META = A_ROWS - 512
BF = jnp.bfloat16
F32 = jnp.float32
I32 = jnp.int32
VMEM_LIMIT = 48 * 1024 * 1024
DN = (((1,), (0,)), ((), ()))


def iota(shape, dim):
    return lax.broadcasted_iota(I32, shape, dim)


def dot(x, y):
    return lax.dot_general(x, y, DN, preferred_element_type=F32)


def to_col(row):
    size = row.shape[1]
    eye = iota((size, size), 0) == iota((size, size), 1)
    spread = jnp.where(eye, jnp.broadcast_to(row.astype(F32), (size, size)), 0.0)
    return jnp.sum(spread, axis=1, keepdims=True).astype(I32)


def ones(mask):
    return jnp.where(mask, 1.0, 0.0)


def ranks(b_row):
    key_row = b_row * 256 + iota(b_row.shape, 1)
    key_col = to_col(key_row)
    rank_row = jnp.sum(ones(key_col < key_row), axis=0, keepdims=True).astype(I32)
    rank_col = jnp.sum(ones(key_row < key_col), axis=1, keepdims=True).astype(I32)
    return rank_row, rank_col, jnp.right_shift(key_col, 8)


def class_counts(labels):
    count = [sum((label == y).astype(I32) for label in labels) for y in range(8)]
    order = [sum([(labels[k] == labels[j]).astype(I32) for k in range(j)], jnp.int32(0)) for j in range(len(labels))]
    return count, order


def pack_kernel(virt, panel_c, panel_d, pair, b_ref, a_ref, amp_ref, eri_ref, x_ref, hot, masked, q_ref, s_ref, m_ref, meta):
    me = lax.axis_index("depth")
    g = [virt[panel_c[j]] ^ virt[panel_d[j]] for j in range(CDS)]
    b_row = b_ref[...]
    rank_row, rank_col, b_col = ranks(b_row)
    same = jnp.logical_and((rank_row & 15) == (rank_col & 15), rank_col < rank_row)
    diff = b_col ^ b_row
    before = [jnp.sum(ones(jnp.logical_and(same, diff == y)), axis=0, keepdims=True) for y in range(8)]

    def places(labels):
        count, order = class_counts(labels)
        count = [c.astype(F32) for c in count]
        for x in range(8):
            s_ref[x : x + 1, :] = sum(count[y ^ x] * before[y] for y in range(8))
        return [s_ref[pl.ds(labels[j], 1), :] + order[j].astype(F32) for j in range(len(labels))]

    real = iota((1, B_PAD), 1) < B_COLS
    out_places = places([pair[me * OWN_IJ + j] for j in range(OWN_IJ)])
    top_out = jnp.max(jnp.where(real, sum_max(out_places), 0.0), axis=1, keepdims=True)
    in_places = places(g)
    top_in = jnp.max(jnp.where(real, sum_max(in_places), 0.0), axis=1, keepdims=True)
    over = jnp.maximum(ones(top_out >= CAP_OUT), ones(top_in >= CAP_IN))
    first = (rank_row & 15) * CAP_IN
    for j in range(CDS):
        q_ref[0:1, j * B_PAD : (j + 1) * B_PAD] = first + in_places[j].astype(I32)
    rows = LAYERS * CAP_IN
    for t in range(CDS * B_PAD // 512):
        at = slice(t * 512, (t + 1) * 512)
        hot[:, at] = ones(iota((rows, 512), 0) == q_ref[0:1, at]).astype(BF)

    masked[...] = jnp.zeros_like(masked)
    ab = (b_col ^ a_ref[...])[:B_COLS, :A_ROWS].astype(F32).astype(BF)
    for j in range(CDS):
        slab = eri_ref[:, j * A_ROWS : (j + 1) * A_ROWS]
        label = jnp.full((1, 1), g[j].astype(F32), F32).astype(BF)
        masked[j * B_PAD : j * B_PAD + B_COLS, 0:A_ROWS] = jnp.where(ab == label, slab, jnp.zeros_like(slab))

    m_ref[...] = jnp.zeros_like(m_ref)
    m_ref[0:8, META : META + CDS] = amp_ref[...].astype(F32)
    lane = iota((1, CDS), 1)
    m_ref[8:9, META : META + CDS] = sum(jnp.where(lane == j, g[j], 0) for j in range(CDS)).astype(F32)
    m_ref[9:10, META : META + CDS] = jnp.broadcast_to(over, (1, CDS))
    meta[...] = jnp.zeros_like(meta)
    for e in range(LAYERS):
        meta[e * CAP_IN : e * CAP_IN + 16, :] = m_ref[...]
    for n in (0, 256):
        x_ref[:, n : n + 256] = dot(hot[...], masked[:, n : n + 256]).astype(BF)
    x_ref[:, 512:640] = (dot(hot[...], masked[:, 512:640]) + meta[...]).astype(BF)


def sum_max(terms):
    top = terms[0]
    for term in terms[1:]:
        top = jnp.maximum(top, term)
    return top


def compute_kernel(b_ref, a_ref, pair_ref, r_ref, y_ref, x_ref, hot, eri, amp, hot2, amps):
    me = lax.axis_index("depth")
    b_row = b_ref[...]
    rank_row, _, _ = ranks(b_row)
    beta = []
    for i in range(PER):
        mine = rank_row == i * LAYERS + me
        beta.append(jnp.sum(jnp.where(mine, b_row, 0).astype(F32), axis=1, keepdims=True).astype(I32))

    g_row = r_ref[0, 8:9, :].astype(F32).astype(I32)
    g_col = to_col(g_row)
    wide = (256, 256)
    same = jnp.right_shift(iota(wide, 0), 4) == jnp.right_shift(iota(wide, 1), 4)
    earlier = jnp.logical_and(same, iota(wide, 1) < iota(wide, 0))
    order = jnp.sum(ones(jnp.logical_and(earlier, g_row == g_col)), axis=1, keepdims=True)
    lane = iota((1, 128), 1)
    part, label = jnp.right_shift(lane, 3), lane & 7
    own = sum(jnp.where(part == i, beta[i], 0) for i in range(PER))
    wanted = (label ^ own) ^ g_col
    seen = sum(ones(jnp.logical_and(part > i, wanted == beta[i])) for i in range(PER - 1))
    count = dot(ones(same).astype(BF), ones(g_col == label).astype(BF))
    square = (128, 128)
    by_part = ones(jnp.right_shift(iota(square, 0), 3) == iota(square, 1)).astype(BF)
    place = dot((seen * count).astype(BF), by_part) + order
    rows = iota((256, 1), 0)
    place = place.astype(I32) + (jnp.right_shift(rows, 4) & 3) * CAP_IN

    four = 4 * CAP_IN
    sym = [a_ref[...] ^ beta[i] for i in range(PER)]
    for k in range(4):
        at = slice(k * 64, (k + 1) * 64)
        for i in range(PER):
            hot[i * 64 : (i + 1) * 64, :] = ones(iota((64, four), 1) == place[at, i : i + 1]).astype(BF)
        for n, w in ((0, 256), (256, 256), (512, 128)):
            got = dot(hot[...], y_ref[k * four : (k + 1) * four, n : n + w])
            for i in range(PER):
                keep = sym[i][:, n : n + w] == g_col[at, :]
                eri[i * 256 + k * 64 : i * 256 + (k + 1) * 64, n : n + w] = jnp.where(
                    keep, got[i * 64 : (i + 1) * 64, :], 0.0
                ).astype(BF)

    p_row = pair_ref[...]
    p_col = to_col(p_row)
    for c in range(LAYERS):
        amps[c * 8 : (c + 1) * 8, :] = r_ref[c, 0:8, :].astype(F32)
    allowed = jnp.where(p_col == g_row, amps[...], 0.0).astype(BF)
    same2 = jnp.right_shift(iota(square, 0), 3) == jnp.right_shift(iota(square, 1), 3)
    earlier2 = jnp.logical_and(same2, iota(square, 0) < iota(square, 1))
    order2 = jnp.sum(ones(jnp.logical_and(earlier2, p_row == p_col)), axis=0, keepdims=True)
    row = iota((128, 1), 0)
    part2, label2 = jnp.right_shift(row, 3), row & 7
    own2 = sum(jnp.where(part2 == i, beta[i], 0) for i in range(PER))
    wanted2 = (label2 ^ own2) ^ p_row
    seen2 = sum(ones(jnp.logical_and(part2 > i, wanted2 == beta[i])) for i in range(PER - 1))
    count2 = dot(ones(label2 == p_row).astype(BF), ones(same2).astype(BF))
    short = (16, 128)
    by_part2 = ones(jnp.right_shift(iota(short, 1), 3) == iota(short, 0)).astype(BF)
    place2 = dot(by_part2, (seen2 * count2).astype(BF)) + order2
    place2 = place2.astype(I32) + jnp.right_shift(iota((1, 128), 1), 3) * CAP_OUT
    out_rows = LAYERS * CAP_OUT
    for i in range(PER):
        hot2[...] = ones(iota((out_rows, 128), 0) == place2[i : i + 1, :]).astype(BF)
        amp[:, i * 256 : (i + 1) * 256] = dot(hot2[...], allowed).astype(BF)
    for n, w in ((0, 256), (256, 256), (512, 128)):
        x_ref[:, n : n + w] = dot(amp[...], eri[:, n : n + w])


def unpack_kernel(pair, b_ref, a_ref, y_ref, o_ref, hot, high, low, j_ref):
    me = lax.axis_index("depth")
    labels = [pair[me * OWN_IJ + j] for j in range(OWN_IJ)]
    count, order = class_counts(labels)
    for y in range(8):
        j_ref[y] = count[y]
    b_row = b_ref[...]
    rank_row, rank_col, b_col = ranks(b_row)
    same = jnp.logical_and((rank_row & 15) == (rank_col & 15), rank_row < rank_col)
    diff = b_col ^ b_row
    before = [jnp.sum(ones(jnp.logical_and(same, diff == y)), axis=1, keepdims=True) for y in range(8)]
    first = (rank_col & 15) * CAP_OUT
    width = LAYERS * CAP_OUT
    for j in range(OWN_IJ):
        place = sum(j_ref[y ^ labels[j]].astype(F32) * before[y] for y in range(8)) + order[j].astype(F32)
        hot[j * B_PAD : (j + 1) * B_PAD, :] = ones(iota((B_PAD, width), 1) == first + place.astype(I32)).astype(BF)
    whole = y_ref[...]
    top = whole.astype(BF)
    high[...] = top
    low[...] = (whole - top.astype(F32)).astype(BF)
    ab = b_col ^ a_ref[...]
    for j in range(OWN_IJ):
        got = dot(hot[j * B_PAD : (j + 1) * B_PAD, :], high[...]) + dot(hot[j * B_PAD : (j + 1) * B_PAD, :], low[...])
        got = jnp.where(ab == labels[j], got, 0.0)
        o_ref[:, j * A_ROWS : (j + 1) * A_ROWS] = got[:B_COLS, :A_ROWS]


VM = pl.BlockSpec(memory_space=pltpu.VMEM)
SM = pl.BlockSpec(memory_space=pltpu.SMEM)


def call(kernel, args, specs, out, scratch, flops, moved):
    return pl.pallas_call(
        kernel,
        out_shape=out,
        in_specs=specs,
        out_specs=VM,
        scratch_shapes=scratch,
        compiler_params=pltpu.CompilerParams(vmem_limit_bytes=VMEM_LIMIT),
        cost_estimate=pl.CostEstimate(flops=flops, bytes_accessed=moved, transcendentals=0),
    )(*args)


def dense(amplitudes, integrals, virt_irrep, pair_irrep, panel_c, panel_d):
    gathered = lax.all_gather(amplitudes, ("row", "col"), axis=0, tiled=True)
    pair_sym = jnp.bitwise_xor(virt_irrep[panel_c], virt_irrep[panel_d])
    keep = pair_irrep[:, None] == pair_sym[None, :]
    allowed = jnp.where(keep, gathered, jnp.zeros_like(gathered))
    own_rows = allowed.shape[0] // LAYERS
    mine = lax.all_to_all(allowed, "depth", split_axis=0, concat_axis=1, tiled=True)
    piece = lax.all_gather(integrals, "depth", axis=1, tiled=True)
    shaped = piece.reshape(B_COLS, piece.shape[1] // A_ROWS, A_ROWS)
    full = jnp.einsum("jc,bca->jba", mine, shaped, preferred_element_type=F32)
    irrep_a = lax.dynamic_slice_in_dim(virt_irrep, lax.axis_index("row") * A_ROWS, A_ROWS, 0)
    irrep_b = lax.dynamic_slice_in_dim(virt_irrep, lax.axis_index("col") * B_COLS, B_COLS, 0)
    irrep_ij = lax.dynamic_slice_in_dim(pair_irrep, lax.axis_index("depth") * own_rows, own_rows, 0)
    ab_sym = jnp.bitwise_xor(irrep_b[:, None], irrep_a[None, :])
    mask = irrep_ij[:, None, None] == ab_sym[None, :, :]
    masked = jnp.where(mask, full, jnp.float32(0.0))
    return jnp.transpose(masked, (1, 0, 2)).reshape(B_COLS, own_rows * A_ROWS)


def body(amplitudes, integrals, virt_irrep, pair_irrep, panel_c, panel_d):
    irrep_a = lax.dynamic_slice_in_dim(virt_irrep, lax.axis_index("row") * A_ROWS, A_ROWS, 0)
    irrep_b = lax.dynamic_slice_in_dim(virt_irrep, lax.axis_index("col") * B_COLS, B_COLS, 0)
    a_row = jnp.pad(irrep_a, (0, A_PAD - A_ROWS), constant_values=64)[None, :]
    b_row = jnp.pad(irrep_b, (0, B_PAD - B_COLS), constant_values=16)[None, :]
    rows = LAYERS * CAP_IN
    sent = call(
        pack_kernel,
        (virt_irrep, panel_c, panel_d, pair_irrep, b_row, a_row, amplitudes, integrals),
        [SM, SM, SM, SM, VM, VM, VM, VM],
        jax.ShapeDtypeStruct((rows, A_PAD), BF),
        [
            pltpu.VMEM((rows, CDS * B_PAD), BF),
            pltpu.VMEM((CDS * B_PAD, A_PAD), BF),
            pltpu.VMEM((8, CDS * B_PAD), I32),
            pltpu.VMEM((8, B_PAD), F32),
            pltpu.VMEM((16, 128), F32),
            pltpu.VMEM((rows, 128), F32),
        ],
        2 * rows * CDS * B_PAD * A_PAD,
        2 * B_COLS * CDS * A_ROWS,
    )
    held = lax.all_to_all(sent.reshape(LAYERS, CAP_IN, A_PAD), "depth", 0, 0, tiled=True)
    small = held[:, 0:16, A_ROWS : A_ROWS + CDS].transpose(1, 0, 2).reshape(16, LAYERS * CDS)
    shared = lax.all_to_all(jnp.broadcast_to(small[None], (16, 16, LAYERS * CDS)), ("row", "col"), 0, 0, tiled=True)
    over = jnp.max(shared[:, 9, :].astype(F32)) > 0.5

    def packed(shared, held):
        out_rows = LAYERS * CAP_OUT
        part = call(
            compute_kernel,
            (b_row, a_row, pair_irrep[None, :], shared, held.reshape(rows, A_PAD)),
            [VM] * 5,
            jax.ShapeDtypeStruct((out_rows, A_PAD), F32),
            [
                pltpu.VMEM((PER * 64, 4 * CAP_IN), BF),
                pltpu.VMEM((PER * 256, A_PAD), BF),
                pltpu.VMEM((out_rows, PER * 256), BF),
                pltpu.VMEM((out_rows, 128), BF),
                pltpu.VMEM((128, 256), F32),
            ],
            2 * PER * 256 * A_PAD * (out_rows + 4 * CAP_IN),
            2 * rows * A_PAD,
        )
        back = lax.all_to_all(part.reshape(LAYERS, CAP_OUT, A_PAD), "depth", 0, 0, tiled=True)
        return call(
            unpack_kernel,
            (pair_irrep, b_row, a_row, back.reshape(out_rows, A_PAD)),
            [SM, VM, VM, VM],
            jax.ShapeDtypeStruct((B_COLS, OWN_IJ * A_ROWS), F32),
            [
                pltpu.VMEM((OWN_IJ * B_PAD, out_rows), BF),
                pltpu.VMEM((out_rows, A_PAD), BF),
                pltpu.VMEM((out_rows, A_PAD), BF),
                pltpu.SMEM((8,), I32),
            ],
            4 * OWN_IJ * B_PAD * out_rows * A_PAD,
            4 * B_COLS * OWN_IJ * A_ROWS,
        )

    def general(shared, held):
        return dense(amplitudes, integrals, virt_irrep, pair_irrep, panel_c, panel_d)

    return lax.cond(over, general, packed, shared, held)


def solution(mesh):
    return jax.shard_map(
        body,
        mesh=mesh,
        in_specs=(
            P(("row", "col"), "depth"),
            P("col", ("row", "depth")),
            P(),
            P(),
            P("depth"),
            P("depth"),
        ),
        out_specs=P("col", ("row", "depth")),
        check_vma=False,
    )
```

time: 421 us -> 91.2 us (0.22)
  waiting for transfers between devices: 236 us -> 8.47 us
  local copies, waits for them, and re-layouts: 114 us -> 2.48 us
  matrix products: 18.5 us -> 0 us
  Pallas kernels: 0 us -> 16.3 us
  blocking collectives: 29 us -> 39.4 us
    all_gather x1 -> x0, waiting for transfers between devices: 230 us -> none  [body(): piece = lax.all_gather(integrals, 'depth', axis=1, tiled=True)]
    reshape x2 -> x0, local copies, waits for them, and re-layouts: 112 us -> none  [the longest x1 109 us: body(): shaped = piece.reshape(b_cols, width, a_rows)]
    all_to_all x0 -> x2, blocking collectives: none -> 39.4 us  [the longest x1 20.6 us: body(): lax.all_to_all(sent.reshape(LAYERS, CAP_IN, A_PAD), 'depth', 0, 0, tiled=...]
    all_gather x1 -> x0, blocking collectives: 29 us -> none  [body(): gathered = lax.all_gather(amplitudes, ('row', 'col'), axis=0, tiled=True)]
    dot_general x1 -> x0, matrix products: 18.5 us -> none  [body(): jnp.einsum('jc,bca->jba', mine, shaped, preferred_element_type=jnp.float32)]
    pallas_call x0 -> x3, Pallas kernels: none -> 16.3 us  [call(): pl.pallas_call(kernel, out_shape=out, in_specs=specs, out_specs=VM, scrat...]
  transfers between devices with their start and end apart: 2 -> 1, of which waited for: 2 -> 1; matrix products, arithmetic and copies ran while one was open for 1% -> 0% of each run, Pallas kernels for 0% -> 0%
where the time goes in v1:
time: 91.2 us; the launch traced here: 90.1 us
  blocking collectives  39.4 us (43%)
  Pallas kernels  16.3 us (18%)
  between operations  14.1 us (15%)
  starting transfers between devices  8.57 us (9%)
  waiting for transfers between devices  8.47 us (9%)
  local copies, waits for them, and re-layouts  2.48 us (3%)
    all_to_all x1, blocking collectives, body(): lax.all_to_all(sent.reshape(LAYERS, CAP_IN, A_PAD), 'depth', 0, 0, tiled=...  20.6 us
    all_to_all x1, blocking collectives, packed(): lax.all_to_all(part.reshape(LAYERS, CAP_OUT, A_PAD), 'depth', 0, 0, tiled...  18.8 us
    pallas_call x3, Pallas kernels, call(): pl.pallas_call(kernel, out_shape=out, in_specs=specs, out_specs=VM, scrat...  16.3 us
    all_to_all x1, starting transfers between devices, body(): lax.all_to_all(jnp.broadcast_to(small[None], (16, 16, LAYERS * CDS)), ('r...  8.57 us
    all_to_all x1, waiting for transfers between devices, body(): lax.all_to_all(jnp.broadcast_to(small[None], (16, 16, LAYERS * CDS)), ('r...  8.47 us
  transfers between devices with their start and end apart: 1, of which 1 were waited for; matrix products, arithmetic and copies ran while one was open for 0% of the time, Pallas kernels for 0%

profile of v1, /device:TPU:2, one launch (start us, length us, event | category | flops | bytes accessed | tf_op | source)
XLA Modules:
  0.0 90.1 jit_solution(15693829932542866808)
XLA Ops:
  6.5 0.8 dynamic_slice.15
  7.3 0.8 dynamic_slice.16
  8.1 0.0 copy-start
  8.1 0.0 copy-start.1
  8.1 0.0 copy-start.2
  8.1 0.0 copy-start.3
  8.1 0.0 copy-start.4
  8.1 5.7 %shard_map.66 = bf16[640,640]{1,0:T(8,128)(2,1)S(1)} custom-call(s32[1200]{0:T(1024)} %virt.1, s32[16]{0:T(128)} %panel_c.1, s32[16]{0:T(128)} %panel_d.1, s32[128]{0:T(128)} %pair.1, s32[1,160]{1,0:T(1,128)S(1)} %bitcast.20, s32[1,640]{1,0:T(1,128)S(1)} %broadcast_in_dim.33.a_ref, bf16[8,16]{1,0:T(8,128)(2,1)} %amp_ref.1, bf16[150,9600]{1,0:T(8,128)(2,1)} %eri_ref.1), custom_call_target="tpu_custom_call" | custom-call | flops 2097152000 | bytes 2880000 | tf_op jit(solution)/shard_map/pallas_call | solution.py:216
  13.9 20.6 %all_to_all.30 = bf16[16,40,640]{2,1,0:T(8,128)(2,1)S(1)} all-to-all(bf16[16,40,640]{2,1,0:T(8,128)(2,1)S(1)} %bitcast.17), channel_id=1, replica_groups=mesh['row'=2,'col'=8,'depth'=16] {'depth'}, dimensions={0} | all-to-all | bytes 1638400 | tf_op jit(solution)/shard_map/all_to_all | solution.py:268
  34.5 0.1 slice_bitcast_fusion
  34.6 0.1 broadcast_in_dim.34
  34.7 0.7 broadcast_in_dim.35
  35.4 8.6 %all-to-all-start.3 = ((bf16[16,16,256]{2,1,0:T(8,128)(2,1)}), bf16[16,16,256]{2,1,0:T(8,128)(2,1)S(1)}, u32[]{:S(2)}, u32[]{:S(2)}) async-start(bf16[16,16,256]{2,1,0:T(8,128)(2,1)} %broadcast_in_dim.35), calls=%async_computation.3 | async-start | bytes 262144 | tf_op jit(solution)/shard_map/all_to_all | solution.py:270
  44.0 8.5 %all-to-all-done.3 = bf16[16,16,256]{2,1,0:T(8,128)(2,1)S(1)} async-done(((bf16[16,16,256]{2,1,0:T(8,128)(2,1)}), bf16[16,16,256]{2,1,0:T(8,128)(2,1)S(1)}, u32[]{:S(2)}, u32[]{:S(2)}) %all-to-all-start.3) | async-done | bytes 131104 | tf_op jit(solution)/shard_map/all_to_all | solution.py:270
  52.4 0.6 slice_reduce_fusion
  53.7 0.0 copy-done
  53.7 0.0 copy-done.1
  53.7 0.0 copy-done.2
  53.7 0.0 copy-done.3
  53.8 0.0 copy-done.4
  53.8 29.5 %conditional.1 = (f32[150,4800]{1,0:T(8,128)}) conditional(s32[]{:T(128)} %convert_element_type.4, (s32[128]{0:T(128)S(1)}, bf16[16,40,640]{2,1,0:T(8,128)(2,1)S(1)}, s32[1,160]{1,0:T(1,128)S(1)}, s32[1,640]{1,0:T(1,128)S(1)}, bf16[16,16,256]{2,1,0:T(8,128)(2,1)S(1)}) %tuple.23, (s32[128]{0:T(128)S(1)}, s32[1200]{0:T(1024)S(1)}, s32[16]{0:T(128)S(1)}, ...), branch_computations={%region_1.2_spmd, %region_2.3_spmd} | conditional | flops 3040870400 | bytes 295254624 | solution.py:309
  53.8 5.2 %branch_0_fun.2 = f32[384,640]{1,0:T(8,128)S(1)} custom-call(s32[1,160]{1,0:T(1,128)S(1)} %get-tuple-element.31.b_ref, s32[1,640]{1,0:T(1,128)S(1)} %get-tuple-element.32.a_ref, s32[1,128]{1,0:T(1,128)S(1)} %bitcast.22, bf16[16,16,256]{2,1,0:T(8,128)(2,1)S(1)} %get-tuple-element.33.r_ref, bf16[640,640]{1,0:T(8,128)(2,1)S(1)} %bitcast.18), custom_call_target="tpu_custom_call" | custom-call | flops 1782579200 | bytes 819200 | tf_op jit(solution)/shard_map/cond/branch_0_fun/pallas_call | solution.py:216
  59.0 18.8 %all_to_all.29 = f32[16,24,640]{2,1,0:T(8,128)S(1)} all-to-all(f32[16,24,640]{2,1,0:T(8,128)S(1)} %bitcast.16), channel_id=1, replica_groups=mesh['row'=2,'col'=8,'depth'=16] {'depth'}, dimensions={0} | all-to-all | bytes 1966080 | tf_op jit(solution)/shard_map/cond/branch_0_fun/all_to_all | solution.py:290
  77.8 5.4 %branch_0_fun.3 = f32[150,4800]{1,0:T(8,128)} custom-call(s32[128]{0:T(128)S(1)} %get-tuple-element.30.pair, s32[1,160]{1,0:T(1,128)S(1)} %get-tuple-element.31.b_ref, s32[1,640]{1,0:T(1,128)S(1)} %get-tuple-element.32.a_ref, f32[384,640]{1,0:T(8,128)S(1)} %bitcast.15), custom_call_target="tpu_custom_call" | custom-call | flops 1258291200 | bytes 2880000 | tf_op jit(solution)/shard_map/cond/branch_0_fun/pallas_call | solution.py:216
  (4 shorter events, 0.0 us)
Async XLA Ops:
  8.1 45.6 %copy-start = (s32[1200]{0:T(1024)S(1)}, s32[1200]{0:T(1024)}, u32[]{:S(2)}) copy-start(s32[1200]{0:T(1024)} %virt.1) | copy-start | bytes 14404
  8.1 45.6 %copy-start.1 = (bf16[8,16]{1,0:T(8,128)(2,1)S(1)}, bf16[8,16]{1,0:T(8,128)(2,1)}, u32[]{:S(2)}) copy-start(bf16[8,16]{1,0:T(8,128)(2,1)} %amp_ref.1) | copy-start | bytes 772
  8.1 45.6 %copy-start.2 = (s32[128]{0:T(128)S(1)}, s32[128]{0:T(128)}, u32[]{:S(2)}) copy-start(s32[128]{0:T(128)} %pair.1) | copy-start | bytes 1540
  8.1 45.6 %copy-start.3 = (s32[16]{0:T(128)S(1)}, s32[16]{0:T(128)}, u32[]{:S(2)}) copy-start(s32[16]{0:T(128)} %panel_c.1) | copy-start | bytes 196
  8.1 45.6 %copy-start.4 = (s32[16]{0:T(128)S(1)}, s32[16]{0:T(128)}, u32[]{:S(2)}) copy-start(s32[16]{0:T(128)} %panel_d.1) | copy-start | bytes 196
  35.4 17.0 %all-to-all-start.3 = ((bf16[16,16,256]{2,1,0:T(8,128)(2,1)}), bf16[16,16,256]{2,1,0:T(8,128)(2,1)S(1)}, u32[]{:S(2)}, u32[]{:S(2)}) async-start(bf16[16,16,256]{2,1,0:T(8,128)(2,1)} %broadcast_in_dim.35), calls=%async_computation.3 | async-start | bytes 262144 | tf_op jit(solution)/shard_map/all_to_all | solution.py:270

commit v2 on v1

v2 whole, which is shorter than its diff:
```python
import jax
import jax.numpy as jnp
from jax import lax
from jax.experimental import pallas as pl
from jax.experimental.pallas import tpu as pltpu
from jax.sharding import PartitionSpec as P

NV = 1200
LAYERS = 16
A_ROWS = 600
B_COLS = 150
A_PAD = 640
B_PAD = 160
CDS = 16
OWN_IJ = 8
CAP_IN = 40
CAP_OUT = 24
PER = 10
TURN = 1280
META = A_ROWS - 512
BF = jnp.bfloat16
F32 = jnp.float32
I32 = jnp.int32
VMEM_LIMIT = 48 * 1024 * 1024
DN = (((1,), (0,)), ((), ()))


def iota(shape, dim):
    return lax.broadcasted_iota(I32, shape, dim)


def dot(x, y):
    return lax.dot_general(x, y, DN, preferred_element_type=F32)


def to_col(row):
    size = row.shape[1]
    eye = iota((size, size), 0) == iota((size, size), 1)
    spread = jnp.where(eye, jnp.broadcast_to(row.astype(F32), (size, size)), 0.0)
    return jnp.sum(spread, axis=1, keepdims=True).astype(I32)


def ones(mask):
    return jnp.where(mask, 1.0, 0.0)


def ranks(b_row):
    key_row = b_row * 256 + iota(b_row.shape, 1)
    key_col = to_col(key_row)
    rank_row = jnp.sum(ones(key_col < key_row), axis=0, keepdims=True).astype(I32)
    rank_col = jnp.sum(ones(key_row < key_col), axis=1, keepdims=True).astype(I32)
    return rank_row, rank_col, jnp.right_shift(key_col, 8)


def irreps(v_ref, turn):
    turn[:, 0:NV] = jnp.broadcast_to(v_ref[...], (8, NV))
    turn[:, NV:] = jnp.zeros((8, TURN - NV), I32)
    whole = turn[...]
    a_at = lax.axis_index("row") * A_ROWS
    b_at = lax.axis_index("col") * B_COLS
    a_row = pltpu.roll(whole, TURN - a_at, 1)[0:1, 0:A_PAD]
    b_row = pltpu.roll(whole, TURN - b_at, 1)[0:1, 0:B_PAD]
    a_row = jnp.where(iota((1, A_PAD), 1) < A_ROWS, a_row, 64)
    return a_row, jnp.where(iota((1, B_PAD), 1) < B_COLS, b_row, 16)


def class_counts(labels):
    count = [sum((label == y).astype(I32) for label in labels) for y in range(8)]
    order = [sum([(labels[k] == labels[j]).astype(I32) for k in range(j)], jnp.int32(0)) for j in range(len(labels))]
    return count, order


def slots(pair_ref):
    p_row = pair_ref[...]
    p_col = to_col(p_row)
    square = (128, 128)
    alike = p_row == p_col
    row = jnp.sum(ones(jnp.logical_and(alike, iota(square, 0) < iota(square, 1))), axis=0, keepdims=True)
    col = jnp.sum(ones(jnp.logical_and(alike, iota(square, 1) < iota(square, 0))), axis=1, keepdims=True)
    return row.astype(I32), col.astype(I32), p_col


def place_kernel(virt, panel, pair, v_ref, pair_ref, q_ref, m_ref, s_ref, turn, each):
    me = lax.axis_index("depth")
    _, b_row = irreps(v_ref, turn)
    g = [virt[panel[j]] ^ virt[panel[CDS + j]] for j in range(CDS)]
    rank_row, rank_col, b_col = ranks(b_row)
    same = jnp.logical_and((rank_row & 15) == (rank_col & 15), rank_col < rank_row)
    diff = b_col ^ b_row
    before = [jnp.sum(ones(jnp.logical_and(same, diff == y)), axis=0, keepdims=True) for y in range(8)]
    count, order = class_counts(g)
    count = [c.astype(F32) for c in count]
    for x in range(8):
        s_ref[x : x + 1, :] = sum(count[y ^ x] * before[y] for y in range(8))
    first = (rank_row & 15) * CAP_IN
    for j in range(CDS):
        place = s_ref[pl.ds(g[j], 1), :] + order[j].astype(F32)
        q_ref[0:1, j * B_PAD : (j + 1) * B_PAD] = first + place.astype(I32)

    own = [pair[me * OWN_IJ + j] for j in range(OWN_IJ)]
    for c in range(8):
        each[c : c + 1, 0:B_COLS] = turn[0:1, c * B_COLS : (c + 1) * B_COLS]
    of_col = each[:, 0:B_COLS]
    chunk = jnp.maximum(15 - iota((8, 128), 1), 0)
    start = jnp.zeros((8, 1), I32)
    dealt = []
    for h in range(8):
        end = start + jnp.sum(ones(of_col == h), axis=1, keepdims=True).astype(I32)
        dealt.append((jnp.right_shift(end + chunk, 4) - jnp.right_shift(start + chunk, 4)).astype(F32))
        start = end
    over = jnp.zeros((8, 128), F32)
    for counts, cap in ((count, CAP_IN), ([c.astype(F32) for c in class_counts(own)[0]], CAP_OUT)):
        for x in range(8):
            stacked = sum(counts[y ^ x] * dealt[y] for y in range(8))
            over = jnp.maximum(over, ones(stacked > cap))
    slot_row, _, _ = slots(pair_ref)
    over = jnp.maximum(jnp.max(over, axis=(0, 1), keepdims=True), ones(jnp.max(slot_row, axis=1, keepdims=True) >= CAP_IN))
    lane = iota((1, CDS), 1)
    m_ref[...] = jnp.zeros_like(m_ref)
    m_ref[0:1, META + CDS : META + 2 * CDS] = sum(jnp.where(lane == j, g[j], 0) for j in range(CDS)).astype(F32)
    m_ref[1:2, META + CDS : META + 2 * CDS] = jnp.broadcast_to(over, (1, CDS))


def pack_kernel(g_ref, v_ref, q_ref, eri_ref, x_ref, hot, masked, turn):
    a_row, b_row = irreps(v_ref, turn)
    b_col = to_col(b_row)
    rows = LAYERS * CAP_IN
    for t in range(CDS * B_PAD // 512):
        at = slice(t * 512, (t + 1) * 512)
        hot[:, at] = ones(iota((rows, 512), 0) == q_ref[0:1, at]).astype(BF)
    masked[...] = jnp.zeros_like(masked)
    ab = (b_col ^ a_row)[:B_COLS, :A_ROWS].astype(F32).astype(BF)
    for j in range(CDS):
        slab = eri_ref[:, j * A_ROWS : (j + 1) * A_ROWS]
        label = g_ref[0:1, META + CDS + j : META + CDS + j + 1].astype(BF)
        masked[j * B_PAD : j * B_PAD + B_COLS, 0:A_ROWS] = jnp.where(ab == label, slab, jnp.zeros_like(slab))
    for n, w in ((0, 256), (256, 256), (512, 128)):
        x_ref[:, n : n + w] = dot(hot[...], masked[:, n : n + w]).astype(BF)


def note_kernel(g_ref, pair_ref, amp_ref, x_in, x_ref, m_ref, amps):
    slot_row, _, p_col = slots(pair_ref)
    g_row = g_ref[0:1, META + CDS : META + 2 * CDS].astype(I32)
    for k in range(16):
        block = (lax.axis_index("row") ^ (k & 1)) * 8 + (lax.axis_index("col") ^ (k >> 1))
        amps[pl.ds(pl.multiple_of(block * 8, 8), 8), :] = amp_ref[k * 8 : (k + 1) * 8, :].astype(F32)
    allowed = jnp.where(p_col == g_row, amps[...], 0.0).astype(BF)
    in_slot = ones(iota((CAP_IN, 128), 0) == slot_row).astype(BF)
    m_ref[...] = g_ref[...]
    m_ref[:, META : META + CDS] = dot(in_slot, allowed)
    note = m_ref[...]
    whole = jnp.concatenate([note] * LAYERS, axis=0)
    x_ref[...] = (x_in[...].astype(F32) + whole).astype(BF)


def compute_kernel(v_ref, pair_ref, r_ref, y_ref, x_ref, hot, eri, amp, hot2, turn):
    me = lax.axis_index("depth")
    a_row, b_row = irreps(v_ref, turn)
    rank_row, _, _ = ranks(b_row)
    beta = []
    for i in range(PER):
        mine = rank_row == i * LAYERS + me
        beta.append(jnp.sum(jnp.where(mine, b_row, 0).astype(F32), axis=1, keepdims=True).astype(I32))

    g_row = r_ref[1, 0:1, :].astype(F32).astype(I32)
    g_col = to_col(g_row)
    wide = (256, 256)
    same = jnp.right_shift(iota(wide, 0), 4) == jnp.right_shift(iota(wide, 1), 4)
    earlier = jnp.logical_and(same, iota(wide, 1) < iota(wide, 0))
    order = jnp.sum(ones(jnp.logical_and(earlier, g_row == g_col)), axis=1, keepdims=True)
    lane = iota((1, 128), 1)
    part, label = jnp.right_shift(lane, 3), lane & 7
    own = sum(jnp.where(part == i, beta[i], 0) for i in range(PER))
    wanted = (label ^ own) ^ g_col
    seen = sum(ones(jnp.logical_and(part > i, wanted == beta[i])) for i in range(PER - 1))
    count = dot(ones(same).astype(BF), ones(g_col == label).astype(BF))
    square = (128, 128)
    by_part = ones(jnp.right_shift(iota(square, 0), 3) == iota(square, 1)).astype(BF)
    place = dot((seen * count).astype(BF), by_part) + order
    rows = iota((256, 1), 0)
    place = place.astype(I32) + (jnp.right_shift(rows, 4) & 3) * CAP_IN

    four = 4 * CAP_IN
    sym = [a_row ^ beta[i] for i in range(PER)]
    for k in range(4):
        at = slice(k * 64, (k + 1) * 64)
        for i in range(PER):
            hot[i * 64 : (i + 1) * 64, :] = ones(iota((64, four), 1) == place[at, i : i + 1]).astype(BF)
        for n, w in ((0, 256), (256, 256), (512, 128)):
            got = dot(hot[...], y_ref[k * four : (k + 1) * four, n : n + w])
            for i in range(PER):
                keep = sym[i][:, n : n + w] == g_col[at, :]
                eri[i * 256 + k * 64 : i * 256 + (k + 1) * 64, n : n + w] = jnp.where(
                    keep, got[i * 64 : (i + 1) * 64, :], 0.0
                ).astype(BF)

    p_row = pair_ref[...]
    _, slot_col, p_col = slots(pair_ref)
    from_slot = ones(iota((128, CAP_IN), 1) == slot_col).astype(BF)
    allowed = jnp.where(p_col == g_row, dot(from_slot, r_ref[0]), 0.0).astype(BF)
    same2 = jnp.right_shift(iota(square, 0), 3) == jnp.right_shift(iota(square, 1), 3)
    earlier2 = jnp.logical_and(same2, iota(square, 0) < iota(square, 1))
    order2 = jnp.sum(ones(jnp.logical_and(earlier2, p_row == p_col)), axis=0, keepdims=True)
    row = iota((128, 1), 0)
    part2, label2 = jnp.right_shift(row, 3), row & 7
    own2 = sum(jnp.where(part2 == i, beta[i], 0) for i in range(PER))
    wanted2 = (label2 ^ own2) ^ p_row
    seen2 = sum(ones(jnp.logical_and(part2 > i, wanted2 == beta[i])) for i in range(PER - 1))
    count2 = dot(ones(label2 == p_row).astype(BF), ones(same2).astype(BF))
    short = (16, 128)
    by_part2 = ones(jnp.right_shift(iota(short, 1), 3) == iota(short, 0)).astype(BF)
    place2 = dot(by_part2, (seen2 * count2).astype(BF)) + order2
    place2 = place2.astype(I32) + (LAYERS - 1 - jnp.right_shift(iota((1, 128), 1), 3)) * CAP_OUT
    out_rows = LAYERS * CAP_OUT
    for i in range(PER):
        hot2[...] = ones(iota((out_rows, 128), 0) == place2[i : i + 1, :]).astype(BF)
        amp[:, i * 256 : (i + 1) * 256] = dot(hot2[...], allowed).astype(BF)
    for n, w in ((0, 256), (256, 256), (512, 128)):
        x_ref[:, n : n + w] = dot(amp[...], eri[:, n : n + w])


def unpack_kernel(pair, v_ref, y_ref, o_ref, hot, high, low, j_ref, turn):
    me = lax.axis_index("depth")
    a_row, b_row = irreps(v_ref, turn)
    labels = [pair[me * OWN_IJ + j] for j in range(OWN_IJ)]
    count, order = class_counts(labels)
    for y in range(8):
        j_ref[y] = count[y]
    rank_row, rank_col, b_col = ranks(b_row)
    same = jnp.logical_and((rank_row & 15) == (rank_col & 15), rank_row < rank_col)
    diff = b_col ^ b_row
    before = [jnp.sum(ones(jnp.logical_and(same, diff == y)), axis=1, keepdims=True) for y in range(8)]
    first = (LAYERS - 1 - (rank_col & 15)) * CAP_OUT
    width = LAYERS * CAP_OUT
    for j in range(OWN_IJ):
        place = sum(j_ref[y ^ labels[j]].astype(F32) * before[y] for y in range(8)) + order[j].astype(F32)
        hot[j * B_PAD : (j + 1) * B_PAD, :] = ones(iota((B_PAD, width), 1) == first + place.astype(I32)).astype(BF)
    whole = y_ref[...]
    top = whole.astype(BF)
    high[...] = top
    low[...] = (whole - top.astype(F32)).astype(BF)
    ab = b_col ^ a_row
    for j in range(OWN_IJ):
        got = dot(hot[j * B_PAD : (j + 1) * B_PAD, :], high[...]) + dot(hot[j * B_PAD : (j + 1) * B_PAD, :], low[...])
        got = jnp.where(ab == labels[j], got, 0.0)
        o_ref[:, j * A_ROWS : (j + 1) * A_ROWS] = got[:B_COLS, :A_ROWS]


VM = pl.BlockSpec(memory_space=pltpu.VMEM)
SM = pl.BlockSpec(memory_space=pltpu.SMEM)


def call(kernel, args, specs, out, scratch, flops, moved):
    return pl.pallas_call(
        kernel,
        out_shape=out,
        in_specs=specs,
        out_specs=[VM] * len(out) if isinstance(out, tuple) else VM,
        scratch_shapes=scratch,
        compiler_params=pltpu.CompilerParams(vmem_limit_bytes=VMEM_LIMIT),
        cost_estimate=pl.CostEstimate(flops=flops, bytes_accessed=moved, transcendentals=0),
    )(*args)


def dense(rows, shared, integrals, virt_irrep, pair_irrep):
    rows = rows.reshape(LAYERS, OWN_IJ, CDS)
    at = jnp.arange(LAYERS)
    at = (lax.axis_index("row") ^ (at >> 3)) + 2 * (lax.axis_index("col") ^ (at & 7))
    amps = jnp.take(rows, at, axis=0).reshape(1, LAYERS * OWN_IJ, CDS)
    amps = jnp.broadcast_to(amps, (LAYERS, LAYERS * OWN_IJ, CDS))
    amps = lax.all_to_all(amps, "depth", 0, 0, tiled=True).transpose(1, 0, 2).reshape(-1, LAYERS * CDS)
    pair_sym = shared[1, 0, :].astype(I32)
    allowed = jnp.where(pair_irrep[:, None] == pair_sym[None, :], amps, jnp.zeros_like(amps))
    share = B_PAD // LAYERS
    padded = jnp.pad(integrals, ((0, B_PAD - B_COLS), (0, 0))).reshape(LAYERS, share, CDS * A_ROWS)
    piece = lax.all_to_all(padded, "depth", 0, 0, tiled=True).reshape(LAYERS, share, CDS, A_ROWS)
    full = jnp.einsum("jsc,sbca->jba", allowed.reshape(-1, LAYERS, CDS), piece, preferred_element_type=F32)
    back = lax.all_to_all(full, "depth", 0, 0, tiled=True).reshape(LAYERS, OWN_IJ, share, A_ROWS)
    mine = back.transpose(0, 2, 1, 3).reshape(B_PAD, OWN_IJ, A_ROWS)[:B_COLS]
    irrep_a = lax.dynamic_slice_in_dim(virt_irrep, lax.axis_index("row") * A_ROWS, A_ROWS, 0)
    irrep_b = lax.dynamic_slice_in_dim(virt_irrep, lax.axis_index("col") * B_COLS, B_COLS, 0)
    irrep_ij = lax.dynamic_slice_in_dim(pair_irrep, lax.axis_index("depth") * OWN_IJ, OWN_IJ, 0)
    ab_sym = jnp.bitwise_xor(irrep_b[:, None], irrep_a[None, :])
    mask = irrep_ij[None, :, None] == ab_sym[:, None, :]
    return jnp.where(mask, mine, jnp.float32(0.0)).reshape(B_COLS, OWN_IJ * A_ROWS)


def swap(array, axis, size, step):
    return lax.ppermute(array, axis, [(d, d ^ step) for d in range(size)])


def body(amplitudes, integrals, virt_irrep, pair_irrep, panel_c, panel_d):
    rows = LAYERS * CAP_IN
    out_rows = LAYERS * CAP_OUT
    p_row = pair_irrep[None, :]
    turn = pltpu.VMEM((8, TURN), I32)
    amps = jnp.concatenate([amplitudes, swap(amplitudes, "row", 2, 1)], axis=0)
    amps, virt_irrep, panel_c, panel_d = lax.optimization_barrier((amps, virt_irrep, panel_c, panel_d))
    near = swap(amps, "col", 8, 1)
    v_row = virt_irrep[None, :]
    panel = jnp.concatenate([panel_c, panel_d])
    near, v_row, panel = lax.optimization_barrier((near, v_row, panel))
    amps = jnp.concatenate([amps, near], axis=0)
    two = swap(amps, "col", 8, 2)
    place, notes = call(
        place_kernel,
        (virt_irrep, panel, pair_irrep, v_row, p_row),
        [SM, SM, SM, VM, VM],
        (jax.ShapeDtypeStruct((8, CDS * B_PAD), I32), jax.ShapeDtypeStruct((CAP_IN, 128), F32)),
        [pltpu.VMEM((8, B_PAD), F32), turn, pltpu.VMEM((8, 256), I32)],
        4 * 10**8,
        10**5,
    )
    two, place = lax.optimization_barrier((two, place))
    amps = jnp.concatenate([amps, two], axis=0)
    amps = jnp.concatenate([amps, swap(amps, "col", 8, 4)], axis=0)
    sent = call(
        pack_kernel,
        (notes, v_row, place, integrals),
        [VM] * 4,
        jax.ShapeDtypeStruct((rows, A_PAD), BF),
        [
            pltpu.VMEM((rows, CDS * B_PAD), BF),
            pltpu.VMEM((CDS * B_PAD, A_PAD), BF),
            turn,
        ],
        2 * rows * CDS * B_PAD * A_PAD,
        2 * B_COLS * CDS * A_ROWS,
    )
    last = pl.BlockSpec((rows, 128), lambda n: (0, A_PAD // 128 - 1))
    sent = pl.pallas_call(
        note_kernel,
        out_shape=jax.ShapeDtypeStruct((rows, A_PAD), BF),
        grid=(1,),
        in_specs=[
            pl.BlockSpec((CAP_IN, 128), lambda n: (0, 0)),
            pl.BlockSpec((1, 128), lambda n: (0, 0)),
            pl.BlockSpec((128, CDS), lambda n: (0, 0)),
            last,
        ],
        out_specs=last,
        scratch_shapes=[pltpu.VMEM((CAP_IN, 128), F32), pltpu.VMEM((128, CDS), F32)],
        input_output_aliases={3: 0},
        compiler_params=pltpu.CompilerParams(vmem_limit_bytes=VMEM_LIMIT),
        cost_estimate=pl.CostEstimate(flops=10**7, bytes_accessed=4 * rows * 128, transcendentals=0),
    )(notes, p_row, amps, sent)
    held = lax.all_to_all(sent.reshape(LAYERS, CAP_IN, A_PAD), "depth", 0, 0, tiled=True)
    shared = held[:, :, A_ROWS : A_ROWS + 2 * CDS].reshape(LAYERS, CAP_IN, 2, CDS)
    shared = shared.transpose(2, 1, 0, 3).reshape(2, CAP_IN, LAYERS * CDS)
    over = jnp.max(shared[1, 1, :].astype(F32)) > 0.5

    def packed(shared, held, amps):
        part = call(
            compute_kernel,
            (v_row, p_row, shared, held.reshape(rows, A_PAD)),
            [VM] * 4,
            jax.ShapeDtypeStruct((out_rows, A_PAD), F32),
            [
                pltpu.VMEM((PER * 64, 4 * CAP_IN), BF),
                pltpu.VMEM((PER * 256, A_PAD), BF),
                pltpu.VMEM((out_rows, PER * 256), BF),
                pltpu.VMEM((out_rows, 128), BF),
                turn,
            ],
            2 * PER * 256 * A_PAD * (out_rows + 4 * CAP_IN),
            2 * rows * A_PAD,
        )
        turned = [list(range(LAYERS - 1, -1, -1))]
        part = part.reshape(LAYERS, CAP_OUT, A_PAD)
        back = lax.all_to_all(part, "depth", 0, 0, tiled=True, axis_index_groups=turned)
        return call(
            unpack_kernel,
            (pair_irrep, v_row, back.reshape(out_rows, A_PAD)),
            [SM, VM, VM],
            jax.ShapeDtypeStruct((B_COLS, OWN_IJ * A_ROWS), F32),
            [
                pltpu.VMEM((OWN_IJ * B_PAD, out_rows), BF),
                pltpu.VMEM((out_rows, A_PAD), BF),
                pltpu.VMEM((out_rows, A_PAD), BF),
                pltpu.SMEM((8,), I32),
                turn,
            ],
            4 * OWN_IJ * B_PAD * out_rows * A_PAD,
            4 * B_COLS * OWN_IJ * A_ROWS,
        )

    def general(shared, held, amps):
        return dense(amps, shared, integrals, virt_irrep, pair_irrep)

    return lax.cond(over, general, packed, shared, held, amps)


def solution(mesh):
    return jax.shard_map(
        body,
        mesh=mesh,
        in_specs=(
            P(("row", "col"), "depth"),
            P("col", ("row", "depth")),
            P(),
            P(),
            P("depth"),
            P("depth"),
        ),
        out_specs=P("col", ("row", "depth")),
        check_vma=False,
    )
```

time: 91.2 us -> 71.3 us (0.78)
  between operations: 14.1 us -> 0.74 us
  waiting for transfers between devices: 8.47 us -> 1.52 us
  blocking collectives: 39.4 us -> 34 us
  starting transfers between devices: 8.57 us -> 12.1 us
  other arithmetic: 0.64 us -> 1.76 us
  local copies, waits for them, and re-layouts: 2.48 us -> 3.53 us
    ppermute x0 -> x4, starting transfers between devices: none -> 12.1 us  [swap(): return lax.ppermute(array, axis, [(d, d ^ step) for d in range(size)])]
    all_to_all x1 -> x0, starting transfers between devices: 8.57 us -> none  [body(): lax.all_to_all(jnp.broadcast_to(small[None], (16, 16, LAYERS * CDS)), ('r...]
    all_to_all x1 -> x0, waiting for transfers between devices: 8.47 us -> none  [body(): lax.all_to_all(jnp.broadcast_to(small[None], (16, 16, LAYERS * CDS)), ('r...]
    all_to_all x1, blocking collectives: 18.8 us -> 15.6 us  [packed(): lax.all_to_all(part, 'depth', 0, 0, tiled=True, axis_index_groups=turned)]
    unnamed x10 -> x8, local copies, waits for them, and re-layouts: 0.03 us -> 2.49 us
    all_to_all x1, blocking collectives: 20.6 us -> 18.4 us  [body(): lax.all_to_all(sent.reshape(LAYERS, CAP_IN, A_PAD), 'depth', 0, 0, tiled=...]
    dynamic_slice x2 -> x0, local copies, waits for them, and re-layouts: 1.54 us -> none  [the longest x1 0.77 us: body(): lax.dynamic_slice_in_dim(virt_irrep, lax.axis_index('col') * B_COLS, B_CO...]
    ppermute x0 -> x4, waiting for transfers between devices: none -> 1.52 us  [swap(): return lax.ppermute(array, axis, [(d, d ^ step) for d in range(size)])]
  transfers between devices with their start and end apart: 1 -> 4, of which waited for: 1 -> 3; matrix products, arithmetic and copies ran while one was open for 0% -> 2% of each run, Pallas kernels for 0% -> 10%
where the time goes in v2:
time: 71.3 us; the launch traced here: 70.6 us
  blocking collectives  34 us (48%)
  Pallas kernels  16.7 us (23%)
  starting transfers between devices  12.1 us (17%)
  local copies, waits for them, and re-layouts  3.53 us (5%)
  other arithmetic  1.76 us (2%)
  waiting for transfers between devices  1.52 us (2%)
  between operations  0.74 us (1%)
    all_to_all x1, blocking collectives, body(): lax.all_to_all(sent.reshape(LAYERS, CAP_IN, A_PAD), 'depth', 0, 0, tiled=...  18.4 us
    pallas_call x4, Pallas kernels, call(): pl.pallas_call(kernel, out_shape=out, in_specs=specs, out_specs=[VM] * le...  16.2 us
    all_to_all x1, blocking collectives, packed(): lax.all_to_all(part, 'depth', 0, 0, tiled=True, axis_index_groups=turned)  15.6 us
    ppermute x4, starting transfers between devices, swap(): return lax.ppermute(array, axis, [(d, d ^ step) for d in range(size)])  12.1 us
    unnamed x8, local copies, waits for them, and re-layouts  2.49 us
    ppermute x4, waiting for transfers between devices, swap(): return lax.ppermute(array, axis, [(d, d ^ step) for d in range(size)])  1.52 us
  transfers between devices with their start and end apart: 4, of which 3 were waited for; matrix products, arithmetic and copies ran while one was open for 2% of the time, Pallas kernels for 10%

profile of v2, /device:TPU:2, one launch (start us, length us, event | category | flops | bytes accessed | tf_op | source)
XLA Modules:
  0.0 70.6 jit_solution(14803028681479809192)
XLA Ops:
  0.0 0.8 %copy.43 = bf16[8,16]{0,1:T(8,128)(2,1)S(1)} copy(bf16[8,16]{1,0:T(8,128)(2,1)} %param.8) | data formatting | bytes 512 | tf_op args[0]
  0.8 0.0 collective-permute-start
  0.8 1.2 %collective-permute-done = bf16[8,16]{0,1:T(8,128)(2,1)S(1)} collective-permute-done((bf16[8,16]{0,1:T(8,128)(2,1)S(1)}, bf16[8,16]{0,1:T(8,128)(2,1)S(1)}, u32[]{:S(2)}, u32[]{:S(2)}) %collective-permute-start) | collective-permute-done | bytes 288 | tf_op jit(solution)/shard_map/ppermute | solution.py:289
  1.9 0.1 pad_maximum_fusion
  2.0 1.9 %collective-permute-start.1 = (bf16[16,16]{0,1:T(8,128)(2,1)S(1)}, bf16[16,16]{0,1:T(8,128)(2,1)S(1)}, u32[]{:S(2)}, u32[]{:S(2)}) collective-permute-start(bf16[16,16]{0,1:T(8,128)(2,1)S(1)} %pad_maximum_fusion), channel_id=1, source_target_pairs={{0,16},{16,0},{32,48},{48,32},{64,80},{80,64},{96,112},{112,96},{1... | collective-permute-start | bytes 1544 | tf_op jit(solution)/shard_map/ppermute | solution.py:289
  3.9 0.7 %pad_add_fusion.panel = s32[32]{0:T(128)S(1)} fusion(s32[16]{0:T(128)} %param.13, s32[16]{0:T(128)} %param.12), kind=kLoop, calls=%fused_computation.25 | loop fusion | flops 32 | bytes 256 | tf_op jit(solution)/shard_map/concatenate | solution.py:301
  4.7 0.7 broadcast_in_dim.35.v_ref
  5.4 0.2 collective-permute-done.1
  5.6 0.1 pad_maximum_fusion.1
  5.7 3.3 %collective-permute-start.2 = (bf16[32,16]{0,1:T(8,128)(2,1)S(1)}, bf16[32,16]{0,1:T(8,128)(2,1)S(1)}, u32[]{:S(2)}, u32[]{:S(2)}) collective-permute-start(bf16[32,16]{0,1:T(8,128)(2,1)S(1)} %pad_maximum_fusion.1), channel_id=1, source_target_pairs={{0,32},{16,48},{32,0},{48,16},{64,96},{80,112},{96,64},{112,80},{1... | collective-permute-start | bytes 3080 | tf_op jit(solution)/shard_map/ppermute | solution.py:289
  9.0 1.5 %shard_map.66 = (s32[8,2560]{1,0:T(8,128)S(1)}, f32[40,128]{1,0:T(8,128)S(1)}) custom-call(s32[1200]{0:T(1024)} %virt, s32[32]{0:T(128)S(1)} %pad_add_fusion.panel, s32[128]{0:T(128)} %pair.1, s32[1,1200]{1,0:T(1,128)S(1)} %broadcast_in_dim.35.v_ref, s32[1,128]{1,0:T(1,128)} %bitcast.47), custom_call_target="tpu_custom_call" | custom-call | flops 400000000 | bytes 100000 | tf_op jit(solution)/shard_map/pallas_call | solution.py:254
  10.5 0.1 collective-permute-done.2
  10.6 0.1 pad_maximum_fusion.2
  10.7 6.9 %collective-permute-start.3 = (bf16[64,16]{0,1:T(8,128)(2,1)S(1)}, bf16[64,16]{0,1:T(8,128)(2,1)S(1)}, u32[]{:S(2)}, u32[]{:S(2)}) collective-permute-start(bf16[64,16]{0,1:T(8,128)(2,1)S(1)} %pad_maximum_fusion.2), channel_id=1, source_target_pairs={{0,64},{16,80},{32,96},{48,112},{64,0},{80,16},{96,32},{112,48},{1... | collective-permute-start | bytes 6152 | tf_op jit(solution)/shard_map/ppermute | solution.py:289
  17.5 0.0 copy-start.1
  17.5 5.3 %shard_map.67.x_in = bf16[640,640]{1,0:T(8,128)(2,1)S(1)} custom-call(f32[40,128]{1,0:T(8,128)S(1)} %get-tuple-element.55.g_ref, s32[1,1200]{1,0:T(1,128)S(1)} %broadcast_in_dim.35.v_ref, s32[8,2560]{1,0:T(8,128)S(1)} %get-tuple-element.59.q_ref, bf16[150,9600]{1,0:T(8,128)(2,1)} %eri_ref.1), custom_call_target="tpu_custom_call" | custom-call | flops 2097152000 | bytes 2880000 | tf_op jit(solution)/shard_map/pallas_call | solution.py:254
  22.8 0.0 copy-start
  22.8 0.0 collective-permute-done.3
  22.8 0.1 pad_maximum_fusion.3
  22.9 0.1 copy.44.amp_ref
  23.0 0.0 copy-done.1
  23.0 0.5 shard_map.68
  23.5 18.4 %all_to_all.22 = bf16[16,40,640]{2,1,0:T(8,128)(2,1)S(1)} all-to-all(bf16[16,40,640]{2,1,0:T(8,128)(2,1)S(1)} %bitcast.37), channel_id=1, replica_groups=mesh['row'=2,'col'=8,'depth'=16] {'depth'}, dimensions={0} | all-to-all | bytes 1638400 | tf_op jit(solution)/shard_map/all_to_all | solution.py:347
  41.9 0.1 slice.21
  42.0 0.1 copy.57
  42.1 0.7 slice_reduce_fusion
  43.5 0.0 copy-done
  43.5 25.5 %conditional.1 = (f32[150,4800]{1,0:T(8,128)S(1)}) conditional(s32[]{:T(128)} %convert_element_type.16, (bf16[16,40,640]{2,1,0:T(8,128)(2,1)S(1)}, s32[1,1200]{1,0:T(1,128)S(1)}, s32[1,128]{1,0:T(1,128)S(1)}, bf16[2,40,256]{1,2,0:T(8,128)(2,1)S(1)}, s32[128]{0:T(128)S(1)}) %tuple.34, (s32[128]{0:T(128)S(1)}, s32[1200]{0:T(1024)S(1)}, ...), branch_computations={%region_1.0_spmd, %region_2.3_spmd} | conditional | flops 3040870400 | bytes 98954808 | solution.py:390
  43.5 0.1 copy.47.r_ref
  43.6 5.6 %branch_0_fun.2 = f32[384,640]{1,0:T(8,128)S(1)} custom-call(s32[1,1200]{1,0:T(1,128)S(1)} %get-tuple-element.29.v_ref, s32[1,128]{1,0:T(1,128)S(1)} %bitcast.50, bf16[2,40,256]{2,1,0:T(8,128)(2,1)S(1)} %copy.47.r_ref, bf16[640,640]{1,0:T(8,128)(2,1)S(1)} %bitcast.44), custom_call_target="tpu_custom_call" | custom-call | flops 1782579200 | bytes 819200 | tf_op jit(solution)/shard_map/cond/branch_0_fun/pallas_call | solution.py:254
  49.2 15.6 %all_to_all.21 = f32[16,24,640]{2,1,0:T(8,128)S(1)} all-to-all(f32[16,24,640]{2,1,0:T(8,128)S(1)} %bitcast.38), channel_id=1, replica_groups={{15,14,13,12,11,10,9,8,7,6,5,4,3,2,1,0},{31,30,29,28,27,26,25,24,23,22,..., dimensions={0} | all-to-all | bytes 1966080 | tf_op jit(solution)/shard_map/cond/branch_0_fun/all_to_all | solution.py:370
  64.9 3.9 %branch_0_fun.3 = f32[150,4800]{1,0:T(8,128)S(1)} custom-call(s32[128]{0:T(128)S(1)} %get-tuple-element.28.pair, s32[1,1200]{1,0:T(1,128)S(1)} %get-tuple-element.29.v_ref, f32[384,640]{1,0:T(8,128)S(1)} %bitcast.39), custom_call_target="tpu_custom_call" | custom-call | flops 1258291200 | bytes 2880000 | tf_op jit(solution)/shard_map/cond/branch_0_fun/pallas_call | solution.py:254
  69.0 0.0 copy-start.2
  69.0 1.6 %copy-done.2 = f32[150,4800]{1,0:T(8,128)} copy-done((f32[150,4800]{1,0:T(8,128)}, f32[150,4800]{1,0:T(8,128)S(1)}, u32[]{:S(2)}) %copy-start.2) | copy-done | bytes 2880024
  (1 shorter events, 0.0 us)
Async XLA Ops:
  0.8 1.2 %collective-permute-start = (bf16[8,16]{0,1:T(8,128)(2,1)S(1)}, bf16[8,16]{0,1:T(8,128)(2,1)S(1)}, u32[]{:S(2)}, u32[]{:S(2)}) collective-permute-start(bf16[8,16]{0,1:T(8,128)(2,1)S(1)} %copy.43), channel_id=1, source_target_pairs={{0,128},{128,0},{1,129},{129,1},{2,130},{130,2},{3,131},{131,3},{4... | collective-permute-start | bytes 776 | tf_op jit(solution)/shard_map/ppermute | solution.py:289
  2.0 3.6 %collective-permute-start.1 = (bf16[16,16]{0,1:T(8,128)(2,1)S(1)}, bf16[16,16]{0,1:T(8,128)(2,1)S(1)}, u32[]{:S(2)}, u32[]{:S(2)}) collective-permute-start(bf16[16,16]{0,1:T(8,128)(2,1)S(1)} %pad_maximum_fusion), channel_id=1, source_target_pairs={{0,16},{16,0},{32,48},{48,32},{64,80},{80,64},{96,112},{112,96},{1... | collective-permute-start | bytes 1544 | tf_op jit(solution)/shard_map/ppermute | solution.py:289
  5.7 4.9 %collective-permute-start.2 = (bf16[32,16]{0,1:T(8,128)(2,1)S(1)}, bf16[32,16]{0,1:T(8,128)(2,1)S(1)}, u32[]{:S(2)}, u32[]{:S(2)}) collective-permute-start(bf16[32,16]{0,1:T(8,128)(2,1)S(1)} %pad_maximum_fusion.1), channel_id=1, source_target_pairs={{0,32},{16,48},{32,0},{48,16},{64,96},{80,112},{96,64},{112,80},{1... | collective-permute-start | bytes 3080 | tf_op jit(solution)/shard_map/ppermute | solution.py:289
  10.7 12.1 %collective-permute-start.3 = (bf16[64,16]{0,1:T(8,128)(2,1)S(1)}, bf16[64,16]{0,1:T(8,128)(2,1)S(1)}, u32[]{:S(2)}, u32[]{:S(2)}) collective-permute-start(bf16[64,16]{0,1:T(8,128)(2,1)S(1)} %pad_maximum_fusion.2), channel_id=1, source_target_pairs={{0,64},{16,80},{32,96},{48,112},{64,0},{80,16},{96,32},{112,48},{1... | collective-permute-start | bytes 6152 | tf_op jit(solution)/shard_map/ppermute | solution.py:289
  17.5 5.5 %copy-start.1 = (s32[128]{0:T(128)S(1)}, s32[128]{0:T(128)}, u32[]{:S(2)}) copy-start(s32[128]{0:T(128)} %pair.1) | copy-start | bytes 1540
  22.8 20.7 %copy-start = (s32[1200]{0:T(1024)S(1)}, s32[1200]{0:T(1024)}, u32[]{:S(2)}) copy-start(s32[1200]{0:T(1024)} %virt) | copy-start | bytes 14404
  69.0 1.6 %copy-start.2 = (f32[150,4800]{1,0:T(8,128)}, f32[150,4800]{1,0:T(8,128)S(1)}, u32[]{:S(2)}) copy-start(f32[150,4800]{1,0:T(8,128)S(1)} %get-tuple-element.111) | copy-start | bytes 8640004

commit v3 on v2

--- a/solution.py
+++ b/solution.py
@@ -1,3 +1,5 @@
+import functools
+
 import jax
 import jax.numpy as jnp
 from jax import lax
@@ -15,13 +17,15 @@
 OWN_IJ = 8
 CAP_IN = 40
 CAP_OUT = 24
+CAP_LOW = 20
+HALF = 80
 PER = 10
 TURN = 1280
 META = A_ROWS - 512
 BF = jnp.bfloat16
 F32 = jnp.float32
 I32 = jnp.int32
-VMEM_LIMIT = 48 * 1024 * 1024
+VMEM_LIMIT = 20 * 1024 * 1024
 DN = (((1,), (0,)), ((), ()))
 
 
@@ -109,12 +113,15 @@
         dealt.append((jnp.right_shift(end + chunk, 4) - jnp.right_shift(start + chunk, 4)).astype(F32))
         start = end
     over = jnp.zeros((8, 128), F32)
-    for counts, cap in ((count, CAP_IN), ([c.astype(F32) for c in class_counts(own)[0]], CAP_OUT)):
-        for x in range(8):
-            stacked = sum(counts[y ^ x] * dealt[y] for y in range(8))
-            over = jnp.maximum(over, ones(stacked > cap))
+    results = [c.astype(F32) for c in class_counts(own)[0]]
+    for x in range(8):
+        stacked = sum(count[y ^ x] * dealt[y] for y in range(8))
+        back = sum(results[y ^ x] * dealt[y] for y in range(8))
+        wrong = jnp.logical_or(stacked > CAP_IN, back > CAP_OUT)
+        over = jnp.maximum(over, jnp.where(wrong, 2.0, ones(back > CAP_LOW)))
     slot_row, _, _ = slots(pair_ref)
-    over = jnp.maximum(jnp.max(over, axis=(0, 1), keepdims=True), ones(jnp.max(slot_row, axis=1, keepdims=True) >= CAP_IN))
+    crowd = jnp.max(slot_row, axis=1, keepdims=True) >= CAP_IN
+    over = jnp.maximum(jnp.max(over, axis=(0, 1), keepdims=True), jnp.where(crowd, 2.0, 0.0))
     lane = iota((1, CDS), 1)
     m_ref[...] = jnp.zeros_like(m_ref)
     m_ref[0:1, META + CDS : META + 2 * CDS] = sum(jnp.where(lane == j, g[j], 0) for j in range(CDS)).astype(F32)
@@ -128,7 +135,9 @@
     for t in range(CDS * B_PAD // 512):
         at = slice(t * 512, (t + 1) * 512)
         hot[:, at] = ones(iota((rows, 512), 0) == q_ref[0:1, at]).astype(BF)
-    masked[...] = jnp.zeros_like(masked)
+    masked[:, 512:A_PAD] = jnp.zeros((CDS * B_PAD, 128), BF)
+    for j in range(CDS):
+        masked[(j + 1) * B_PAD - 16 : (j + 1) * B_PAD, 0:512] = jnp.zeros((16, 512), BF)
     ab = (b_col ^ a_row)[:B_COLS, :A_ROWS].astype(F32).astype(BF)
     for j in range(CDS):
         slab = eri_ref[:, j * A_ROWS : (j + 1) * A_ROWS]
@@ -153,8 +162,14 @@
     x_ref[...] = (x_in[...].astype(F32) + whole).astype(BF)
 
 
-def compute_kernel(v_ref, pair_ref, r_ref, y_ref, x_ref, hot, eri, amp, hot2, turn):
+def compute_kernel(v_ref, pair_ref, y_ref, x_ref, pair_out, over_ref, hot, eri, amp, hot2, turn, notes, tail, stage):
     me = lax.axis_index("depth")
+    tail[...] = y_ref[:, A_PAD - 128 : A_PAD].astype(F32)
+    for c in range(LAYERS):
+        at = slice(c * CDS, (c + 1) * CDS)
+        notes[0:CAP_IN, at] = tail[c * CAP_IN : (c + 1) * CAP_IN, META : META + CDS]
+        notes[CAP_IN : CAP_IN + 8, at] = tail[c * CAP_IN : c * CAP_IN + 8, META + CDS : META + 2 * CDS]
+    over_ref[0] = jnp.max(notes[CAP_IN + 1 : CAP_IN + 2, :]).astype(I32)
     a_row, b_row = irreps(v_ref, turn)
     rank_row, _, _ = ranks(b_row)
     beta = []
@@ -162,7 +177,7 @@
         mine = rank_row == i * LAYERS + me
         beta.append(jnp.sum(jnp.where(mine, b_row, 0).astype(F32), axis=1, keepdims=True).astype(I32))
 
-    g_row = r_ref[1, 0:1, :].astype(F32).astype(I32)
+    g_row = notes[CAP_IN : CAP_IN + 1, :].astype(I32)
     g_col = to_col(g_row)
     wide = (256, 256)
     same = jnp.right_shift(iota(wide, 0), 4) == jnp.right_shift(iota(wide, 1), 4)
@@ -197,7 +212,7 @@
     p_row = pair_ref[...]
     _, slot_col, p_col = slots(pair_ref)
     from_slot = ones(iota((128, CAP_IN), 1) == slot_col).astype(BF)
-    allowed = jnp.where(p_col == g_row, dot(from_slot, r_ref[0]), 0.0).astype(BF)
+    allowed = jnp.where(p_col == g_row, dot(from_slot, notes[0:CAP_IN, :].astype(BF)), 0.0).astype(BF)
     same2 = jnp.right_shift(iota(square, 0), 3) == jnp.right_shift(iota(square, 1), 3)
     earlier2 = jnp.logical_and(same2, iota(square, 0) < iota(square, 1))
     order2 = jnp.sum(ones(jnp.logical_and(earlier2, p_row == p_col)), axis=0, keepdims=True)
@@ -216,60 +231,84 @@
         hot2[...] = ones(iota((out_rows, 128), 0) == place2[i : i + 1, :]).astype(BF)
         amp[:, i * 256 : (i + 1) * 256] = dot(hot2[...], allowed).astype(BF)
     for n, w in ((0, 256), (256, 256), (512, 128)):
-        x_ref[:, n : n + w] = dot(amp[...], eri[:, n : n + w])
-
-
-def unpack_kernel(pair, v_ref, y_ref, o_ref, hot, high, low, j_ref, turn):
+        got = dot(amp[...], eri[:, n : n + w])
+        x_ref[:, n : n + w] = got
+        high = got.astype(BF).astype(F32)
+        low = got - high
+        for k in range(LAYERS):
+            at = slice(k * CAP_OUT, k * CAP_OUT + CAP_LOW)
+            stage[k * CAP_IN : k * CAP_IN + CAP_LOW, 0:w] = high[at, :]
+            stage[k * CAP_IN + CAP_LOW : (k + 1) * CAP_IN, 0:w] = low[at, :]
+        pair_out[:, n : n + w] = stage[:, 0:w].astype(BF)
+
+
+def unpack_kernel(stride, gap, pair, v_ref, y_ref, o_ref, hot, both, sym, j_ref, turn):
+    step = pl.program_id(0)
     me = lax.axis_index("depth")
-    a_row, b_row = irreps(v_ref, turn)
     labels = [pair[me * OWN_IJ + j] for j in range(OWN_IJ)]
-    count, order = class_counts(labels)
-    for y in range(8):
-        j_ref[y] = count[y]
-    rank_row, rank_col, b_col = ranks(b_row)
-    same = jnp.logical_and((rank_row & 15) == (rank_col & 15), rank_row < rank_col)
-    diff = b_col ^ b_row
-    before = [jnp.sum(ones(jnp.logical_and(same, diff == y)), axis=1, keepdims=True) for y in range(8)]
-    first = (LAYERS - 1 - (rank_col & 15)) * CAP_OUT
-    width = LAYERS * CAP_OUT
-    for j in range(OWN_IJ):
-        place = sum(j_ref[y ^ labels[j]].astype(F32) * before[y] for y in range(8)) + order[j].astype(F32)
-        hot[j * B_PAD : (j + 1) * B_PAD, :] = ones(iota((B_PAD, width), 1) == first + place.astype(I32)).astype(BF)
-    whole = y_ref[...]
-    top = whole.astype(BF)
-    high[...] = top
-    low[...] = (whole - top.astype(F32)).astype(BF)
-    ab = b_col ^ a_row
-    for j in range(OWN_IJ):
-        got = dot(hot[j * B_PAD : (j + 1) * B_PAD, :], high[...]) + dot(hot[j * B_PAD : (j + 1) * B_PAD, :], low[...])
-        got = jnp.where(ab == labels[j], got, 0.0)
-        o_ref[:, j * A_ROWS : (j + 1) * A_ROWS] = got[:B_COLS, :A_ROWS]
+    width = hot.shape[1]
+
+    @pl.when(step == 0)
+    def _():
+        a_row, b_row = irreps(v_ref, turn)
+        count, order = class_counts(labels)
+        for y in range(8):
+            j_ref[y] = count[y]
+        rank_row, rank_col, b_col = ranks(b_row)
+        same = jnp.logical_and((rank_row & 15) == (rank_col & 15), rank_row < rank_col)
+        diff = b_col ^ b_row
+        before = [jnp.sum(ones(jnp.logical_and(same, diff == y)), axis=1, keepdims=True) for y in range(8)]
+        first = (LAYERS - 1 - (rank_col & 15)) * stride
+        for j in range(OWN_IJ):
+            place = sum(j_ref[y ^ labels[j]].astype(F32) * before[y] for y in range(8)) + order[j].astype(F32)
+            place = first + place.astype(I32)
+            for t in range(2):
+                mine = place[t * HALF : (t + 1) * HALF, :]
+                lane = iota((HALF, width), 1)
+                at = (t * OWN_IJ + j) * HALF
+                hot[at : at + HALF, :] = ones(jnp.logical_or(lane == mine, lane == mine + gap)).astype(BF)
+        sym[...] = b_col ^ a_row
+        if y_ref.dtype == F32:
+            whole = y_ref[...]
+            top = whole.astype(BF)
+            both[0:gap, :] = top
+            both[gap : 2 * gap, :] = (whole - top.astype(F32)).astype(BF)
+
+    terms = both if y_ref.dtype == F32 else y_ref
+    rows = OWN_IJ * HALF
+    of_step = hot[pl.ds(pl.multiple_of(step * rows, rows), rows), :]
+    ab = sym[pl.ds(pl.multiple_of(step * HALF, HALF), HALF), :]
+    for n, w, real in ((0, 256, 256), (256, 256, 256), (512, 128, A_ROWS - 512)):
+        got = dot(of_step, terms[:, n : n + w])
+        for j in range(OWN_IJ):
+            part = jnp.where(ab[:, n : n + w] == labels[j], got[j * HALF : (j + 1) * HALF, :], 0.0)
+            o_ref[:, j * A_ROWS + n : j * A_ROWS + n + real] = part[:, :real]
 
 
 VM = pl.BlockSpec(memory_space=pltpu.VMEM)
 SM = pl.BlockSpec(memory_space=pltpu.SMEM)
 
 
-def call(kernel, args, specs, out, scratch, flops, moved):
+def call(kernel, args, specs, out, scratch, flops, moved, outs=VM):
     return pl.pallas_call(
         kernel,
         out_shape=out,
         in_specs=specs,
-        out_specs=[VM] * len(out) if isinstance(out, tuple) else VM,
+        out_specs=outs,
         scratch_shapes=scratch,
         compiler_params=pltpu.CompilerParams(vmem_limit_bytes=VMEM_LIMIT),
         cost_estimate=pl.CostEstimate(flops=flops, bytes_accessed=moved, transcendentals=0),
     )(*args)
 
 
-def dense(rows, shared, integrals, virt_irrep, pair_irrep):
+def dense(rows, held, integrals, virt_irrep, pair_irrep):
     rows = rows.reshape(LAYERS, OWN_IJ, CDS)
     at = jnp.arange(LAYERS)
     at = (lax.axis_index("row") ^ (at >> 3)) + 2 * (lax.axis_index("col") ^ (at & 7))
     amps = jnp.take(rows, at, axis=0).reshape(1, LAYERS * OWN_IJ, CDS)
     amps = jnp.broadcast_to(amps, (LAYERS, LAYERS * OWN_IJ, CDS))
     amps = lax.all_to_all(amps, "depth", 0, 0, tiled=True).transpose(1, 0, 2).reshape(-1, LAYERS * CDS)
-    pair_sym = shared[1, 0, :].astype(I32)
+    pair_sym = held[:, 0, A_ROWS + CDS : A_ROWS + 2 * CDS].reshape(-1).astype(I32)
     allowed = jnp.where(pair_irrep[:, None] == pair_sym[None, :], amps, jnp.zeros_like(amps))
     share = B_PAD // LAYERS
     padded = jnp.pad(integrals, ((0, B_PAD - B_COLS), (0, 0))).reshape(LAYERS, share, CDS * A_ROWS)
@@ -310,6 +349,7 @@
         [pltpu.VMEM((8, B_PAD), F32), turn, pltpu.VMEM((8, 256), I32)],
         4 * 10**8,
         10**5,
+        (VM, VM),
     )
     two, place = lax.optimization_barrier((two, place))
     amps = jnp.concatenate([amps, two], axis=0)
@@ -345,49 +385,69 @@
         cost_estimate=pl.CostEstimate(flops=10**7, bytes_accessed=4 * rows * 128, transcendentals=0),
     )(notes, p_row, amps, sent)
     held = lax.all_to_all(sent.reshape(LAYERS, CAP_IN, A_PAD), "depth", 0, 0, tiled=True)
-    shared = held[:, :, A_ROWS : A_ROWS + 2 * CDS].reshape(LAYERS, CAP_IN, 2, CDS)
-    shared = shared.transpose(2, 1, 0, 3).reshape(2, CAP_IN, LAYERS * CDS)
-    over = jnp.max(shared[1, 1, :].astype(F32)) > 0.5
-
-    def packed(shared, held, amps):
-        part = call(
-            compute_kernel,
-            (v_row, p_row, shared, held.reshape(rows, A_PAD)),
-            [VM] * 4,
+    part, terms, over = call(
+        compute_kernel,
+        (v_row, p_row, held.reshape(rows, A_PAD)),
+        [VM] * 3,
+        (
             jax.ShapeDtypeStruct((out_rows, A_PAD), F32),
-            [
-                pltpu.VMEM((PER * 64, 4 * CAP_IN), BF),
-                pltpu.VMEM((PER * 256, A_PAD), BF),
-                pltpu.VMEM((out_rows, PER * 256), BF),
-                pltpu.VMEM((out_rows, 128), BF),
-                turn,
-            ],
-            2 * PER * 256 * A_PAD * (out_rows + 4 * CAP_IN),
-            2 * rows * A_PAD,
-        )
-        turned = [list(range(LAYERS - 1, -1, -1))]
-        part = part.reshape(LAYERS, CAP_OUT, A_PAD)
-        back = lax.all_to_all(part, "depth", 0, 0, tiled=True, axis_index_groups=turned)
-        return call(
-            unpack_kernel,
-            (pair_irrep, v_row, back.reshape(out_rows, A_PAD)),
-            [SM, VM, VM],
-            jax.ShapeDtypeStruct((B_COLS, OWN_IJ * A_ROWS), F32),
-            [
-                pltpu.VMEM((OWN_IJ * B_PAD, out_rows), BF),
-                pltpu.VMEM((out_rows, A_PAD), BF),
-                pltpu.VMEM((out_rows, A_PAD), BF),
+            jax.ShapeDtypeStruct((rows, A_PAD), BF),
+            jax.ShapeDtypeStruct((1,), I32),
+        ),
+        [
+            pltpu.VMEM((PER * 64, 4 * CAP_IN), BF),
+            pltpu.VMEM((PER * 256, A_PAD), BF),
+            pltpu.VMEM((out_rows, PER * 256), BF),
+            pltpu.VMEM((out_rows, 128), BF),
+            turn,
+            pltpu.VMEM((CAP_IN + 8, LAYERS * CDS), F32),
+            pltpu.VMEM((rows, 128), F32),
+            pltpu.VMEM((rows, 256), F32),
+        ],
+        2 * PER * 256 * A_PAD * (out_rows + 4 * CAP_IN),
+        2 * rows * A_PAD,
+        (VM, VM, SM),
+    )
+
+    turned = [list(range(LAYERS - 1, -1, -1))]
+
+    def finish(array, stride, gap):
+        chunks = array.reshape(LAYERS, stride, A_PAD)
+        back = lax.all_to_all(chunks, "depth", 0, 0, tiled=True, axis_index_groups=turned)
+        back = back.reshape(array.shape)
+        width = 2 * gap if array.dtype == F32 else array.shape[0]
+        whole = lambda shape: pl.BlockSpec(shape, lambda t: (0, 0))
+        return pl.pallas_call(
+            functools.partial(unpack_kernel, stride, gap),
+            out_shape=jax.ShapeDtypeStruct((B_COLS, OWN_IJ * A_ROWS), F32),
+            grid=(2,),
+            in_specs=[SM, whole((1, NV)), whole(array.shape)],
+            out_specs=pl.BlockSpec((HALF, OWN_IJ * A_ROWS), lambda t: (t, 0)),
+            scratch_shapes=[
+                pltpu.VMEM((2 * OWN_IJ * HALF, width), BF),
+                pltpu.VMEM((width if array.dtype == F32 else 16, A_PAD), BF),
+                pltpu.VMEM((B_PAD, A_PAD), I32),
                 pltpu.SMEM((8,), I32),
                 turn,
             ],
-            4 * OWN_IJ * B_PAD * out_rows * A_PAD,
-            4 * B_COLS * OWN_IJ * A_ROWS,
-        )
-
-    def general(shared, held, amps):
-        return dense(amps, shared, integrals, virt_irrep, pair_irrep)
-
-    return lax.cond(over, general, packed, shared, held, amps)
+            compiler_params=pltpu.CompilerParams(vmem_limit_bytes=VMEM_LIMIT),
+            cost_estimate=pl.CostEstimate(
+                flops=4 * OWN_IJ * HALF * width * A_PAD,
+                bytes_accessed=4 * B_COLS * OWN_IJ * A_ROWS,
+                transcendentals=0,
+            ),
+        )(pair_irrep, v_row, back)
+
+    def usual(part, terms, held, amps):
+        return finish(terms, CAP_IN, CAP_LOW)
+
+    def fuller(part, terms, held, amps):
+        return finish(part, CAP_OUT, out_rows)
+
+    def general(part, terms, held, amps):
+        return dense(amps, held, integrals, virt_irrep, pair_irrep)
+
+    return lax.switch(over[0], (usual, fuller, general), part, terms, held, amps)
 
 
 def solution(mesh):

time: 71.3 us -> 68.2 us (0.957)
  local copies, waits for them, and re-layouts: 3.53 us -> 1.59 us
  Pallas kernels: 16.7 us -> 18.1 us
  blocking collectives: 34 us -> 32.7 us
    unnamed x8 -> x7, local copies, waits for them, and re-layouts: 2.49 us -> 0.77 us
    pallas_call x4, Pallas kernels: 16.2 us -> 17.6 us  [the longest x3 12.5 us: call(): pl.pallas_call(kernel, out_shape=out, in_specs=specs, out_specs=outs, scr...]
    all_to_all x1, blocking collectives: 15.6 us -> 14.3 us  [finish(): lax.all_to_all(chunks, 'depth', 0, 0, tiled=True, axis_index_groups=turned)]
  transfers between devices with their start and end apart: 4 -> 4, of which waited for: 3 -> 2; matrix products, arithmetic and copies ran while one was open for 2% -> 2% of each run, Pallas kernels for 10% -> 10%
where the time goes in v3:
time: 68.2 us; the launch traced here: 67.7 us
  blocking collectives  32.7 us (48%)
  Pallas kernels  18.1 us (27%)
  starting transfers between devices  12.1 us (18%)
  local copies, waits for them, and re-layouts  1.59 us (2%)
  waiting for transfers between devices  1.45 us (2%)
  other arithmetic  1.06 us (2%)
  between operations  0.71 us (1%)
    all_to_all x1, blocking collectives, body(): lax.all_to_all(sent.reshape(LAYERS, CAP_IN, A_PAD), 'depth', 0, 0, tiled=...  18.4 us
    all_to_all x1, blocking collectives, finish(): lax.all_to_all(chunks, 'depth', 0, 0, tiled=True, axis_index_groups=turned)  14.3 us
    pallas_call x3, Pallas kernels, call(): pl.pallas_call(kernel, out_shape=out, in_specs=specs, out_specs=outs, scr...  12.5 us
    ppermute x4, starting transfers between devices, swap(): return lax.ppermute(array, axis, [(d, d ^ step) for d in range(size)])  12.1 us
    pallas_call x1, Pallas kernels, finish(): pl.pallas_call(functools.partial(unpack_kernel, stride, gap), out_shape=j...  5.08 us
    ppermute x4, waiting for transfers between devices, swap(): return lax.ppermute(array, axis, [(d, d ^ step) for d in range(size)])  1.45 us
  transfers between devices with their start and end apart: 4, of which 2 were waited for; matrix products, arithmetic and copies ran while one was open for 2% of the time, Pallas kernels for 10%

profile of v3, /device:TPU:2, one launch (start us, length us, event | category | flops | bytes accessed | tf_op | source)
XLA Modules:
  0.0 67.7 jit_solution(13527966310451320002)
XLA Ops:
  0.0 0.8 %copy.36 = bf16[8,16]{0,1:T(8,128)(2,1)S(1)} copy(bf16[8,16]{1,0:T(8,128)(2,1)} %param.9) | data formatting | bytes 512 | tf_op args[0]
  0.8 0.0 collective-permute-start
  0.8 1.2 %collective-permute-done = bf16[8,16]{0,1:T(8,128)(2,1)S(1)} collective-permute-done((bf16[8,16]{0,1:T(8,128)(2,1)S(1)}, bf16[8,16]{0,1:T(8,128)(2,1)S(1)}, u32[]{:S(2)}, u32[]{:S(2)}) %collective-permute-start) | collective-permute-done | bytes 288 | tf_op jit(solution)/shard_map/ppermute | solution.py:328
  1.9 0.1 pad_maximum_fusion
  2.0 1.9 %collective-permute-start.1 = (bf16[16,16]{0,1:T(8,128)(2,1)S(1)}, bf16[16,16]{0,1:T(8,128)(2,1)S(1)}, u32[]{:S(2)}, u32[]{:S(2)}) collective-permute-start(bf16[16,16]{0,1:T(8,128)(2,1)S(1)} %pad_maximum_fusion), channel_id=1, source_target_pairs={{0,16},{16,0},{32,48},{48,32},{64,80},{80,64},{96,112},{112,96},{1... | collective-permute-start | bytes 1544 | tf_op jit(solution)/shard_map/ppermute | solution.py:328
  3.9 0.7 %pad_add_fusion.panel = s32[32]{0:T(128)S(1)} fusion(s32[16]{0:T(128)} %param.14, s32[16]{0:T(128)} %param.13), kind=kLoop, calls=%fused_computation.24 | loop fusion | flops 32 | bytes 256 | tf_op jit(solution)/shard_map/concatenate | solution.py:340
  4.7 0.7 %broadcast_in_dim.35.v_ref = s32[1,1200]{1,0:T(1,128)S(1)} reshape(s32[1200]{0:T(1024)} %virt) | data formatting | bytes 9600 | tf_op jit(solution)/shard_map/broadcast_in_dim | solution.py:339
  5.4 0.2 collective-permute-done.1
  5.6 0.1 pad_maximum_fusion.1
  5.7 3.3 %collective-permute-start.2 = (bf16[32,16]{0,1:T(8,128)(2,1)S(1)}, bf16[32,16]{0,1:T(8,128)(2,1)S(1)}, u32[]{:S(2)}, u32[]{:S(2)}) collective-permute-start(bf16[32,16]{0,1:T(8,128)(2,1)S(1)} %pad_maximum_fusion.1), channel_id=1, source_target_pairs={{0,32},{16,48},{32,0},{48,16},{64,96},{80,112},{96,64},{112,80},{1... | collective-permute-start | bytes 3080 | tf_op jit(solution)/shard_map/ppermute | solution.py:328
  9.0 1.5 %shard_map.67 = (s32[8,2560]{1,0:T(8,128)S(1)}, f32[40,128]{1,0:T(8,128)S(1)}) custom-call(s32[1200]{0:T(1024)} %virt, s32[32]{0:T(128)S(1)} %pad_add_fusion.panel, s32[128]{0:T(128)} %pair.1, s32[1,1200]{1,0:T(1,128)S(1)} %broadcast_in_dim.35.v_ref, s32[1,128]{1,0:T(1,128)} %bitcast.49), custom_call_target="tpu_custom_call" | custom-call | flops 400000000 | bytes 100000 | tf_op jit(solution)/shard_map/pallas_call | solution.py:293
  10.6 0.0 collective-permute-done.2
  10.6 0.1 pad_maximum_fusion.2
  10.7 6.9 %collective-permute-start.3 = (bf16[64,16]{0,1:T(8,128)(2,1)S(1)}, bf16[64,16]{0,1:T(8,128)(2,1)S(1)}, u32[]{:S(2)}, u32[]{:S(2)}) collective-permute-start(bf16[64,16]{0,1:T(8,128)(2,1)S(1)} %pad_maximum_fusion.2), channel_id=1, source_target_pairs={{0,64},{16,80},{32,96},{48,112},{64,0},{80,16},{96,32},{112,48},{1... | collective-permute-start | bytes 6152 | tf_op jit(solution)/shard_map/ppermute | solution.py:328
  17.5 0.0 copy-start.4
  17.5 5.3 %shard_map.68.x_in = bf16[640,640]{1,0:T(8,128)(2,1)S(1)} custom-call(f32[40,128]{1,0:T(8,128)S(1)} %get-tuple-element.62.g_ref, s32[1,1200]{1,0:T(1,128)S(1)} %broadcast_in_dim.35.v_ref, s32[8,2560]{1,0:T(8,128)S(1)} %get-tuple-element.66.q_ref, bf16[150,9600]{1,0:T(8,128)(2,1)} %eri_ref.1), custom_call_target="tpu_custom_call" | custom-call | flops 2097152000 | bytes 2880000 | tf_op jit(solution)/shard_map/pallas_call | solution.py:293
  22.8 0.0 collective-permute-done.3
  22.8 0.1 pad_maximum_fusion.3
  22.9 0.1 copy.37.amp_ref
  23.0 0.0 copy-done.4
  23.0 0.5 shard_map.69
  23.5 18.4 %all_to_all.27 = bf16[16,40,640]{2,1,0:T(8,128)(2,1)S(1)} all-to-all(bf16[16,40,640]{2,1,0:T(8,128)(2,1)S(1)} %bitcast.41), channel_id=1, replica_groups=mesh['row'=2,'col'=8,'depth'=16] {'depth'}, dimensions={0} | all-to-all | bytes 1638400 | tf_op jit(solution)/shard_map/all_to_all | solution.py:387
  41.9 0.0 copy-start.2
  41.9 0.0 copy-start.3
  41.9 5.7 %shard_map.70 = (f32[384,640]{1,0:T(8,128)S(1)}, bf16[640,640]{1,0:T(8,128)(2,1)S(1)}, s32[1]{0:T(128)}) custom-call(s32[1,1200]{1,0:T(1,128)S(1)} %broadcast_in_dim.35.v_ref, s32[1,128]{1,0:T(1,128)S(1)} %bitcast.51, bf16[640,640]{1,0:T(8,128)(2,1)S(1)} %bitcast.45), custom_call_target="tpu_custom_call" | custom-call | flops 1782579200 | bytes 819200 | tf_op jit(solution)/shard_map/pallas_call | solution.py:293
  48.2 0.0 copy-done.2
  48.2 0.0 copy-done.3
  48.2 19.4 %conditional.1 = (f32[150,4800]{1,0:T(8,128)}) conditional(s32[]{:T(128)} %bitcast.17, (bf16[640,640]{1,0:T(8,128)(2,1)S(1)}, s32[128]{0:T(128)S(1)}, s32[1,1200]{1,0:T(1,128)S(1)}) %tuple.33, (f32[384,640]{1,0:T(8,128)S(1)}, s32[128]{0:T(128)S(1)}, s32[1,1200]{1,0:T(1,128)S(1)}) %tuple.34, (s32[128]{0:T(128)S(1)}, ...), branch_computations={%region_0.0_spmd, %region_1.0_spmd, %region_2.3_spmd} | conditional | flops 1258291200 | bytes 107062904 | solution.py:450
  48.3 14.3 %all_to_all.25 = bf16[16,40,640]{2,1,0:T(8,128)(2,1)S(1)} all-to-all(bf16[16,40,640]{2,1,0:T(8,128)(2,1)S(1)} %bitcast.47), channel_id=1, replica_groups={{15,14,13,12,11,10,9,8,7,6,5,4,3,2,1,0},{31,30,29,28,27,26,25,24,23,22,..., dimensions={0} | all-to-all | bytes 1638400 | tf_op jit(solution)/shard_map/cond/branch_0_fun/all_to_all | solution.py:416
  62.6 5.1 %branch_0_fun.1 = f32[150,4800]{1,0:T(8,128)} custom-call(s32[128]{0:T(128)S(1)} %get-tuple-element.30.pair, s32[1,1200]{1,0:T(1,128)S(1)} %get-tuple-element.32.v_ref, bf16[640,640]{1,0:T(8,128)(2,1)S(1)} %bitcast.43), custom_call_target="tpu_custom_call" | custom-call | flops 1048576000 | bytes 2880000 | tf_op jit(solution)/shard_map/cond/branch_0_fun/pallas_call | solution.py:420
Async XLA Ops:
  0.8 1.2 %collective-permute-start = (bf16[8,16]{0,1:T(8,128)(2,1)S(1)}, bf16[8,16]{0,1:T(8,128)(2,1)S(1)}, u32[]{:S(2)}, u32[]{:S(2)}) collective-permute-start(bf16[8,16]{0,1:T(8,128)(2,1)S(1)} %copy.36), channel_id=1, source_target_pairs={{0,128},{128,0},{1,129},{129,1},{2,130},{130,2},{3,131},{131,3},{4... | collective-permute-start | bytes 776 | tf_op jit(solution)/shard_map/ppermute | solution.py:328
  2.0 3.6 %collective-permute-start.1 = (bf16[16,16]{0,1:T(8,128)(2,1)S(1)}, bf16[16,16]{0,1:T(8,128)(2,1)S(1)}, u32[]{:S(2)}, u32[]{:S(2)}) collective-permute-start(bf16[16,16]{0,1:T(8,128)(2,1)S(1)} %pad_maximum_fusion), channel_id=1, source_target_pairs={{0,16},{16,0},{32,48},{48,32},{64,80},{80,64},{96,112},{112,96},{1... | collective-permute-start | bytes 1544 | tf_op jit(solution)/shard_map/ppermute | solution.py:328
  5.7 4.9 %collective-permute-start.2 = (bf16[32,16]{0,1:T(8,128)(2,1)S(1)}, bf16[32,16]{0,1:T(8,128)(2,1)S(1)}, u32[]{:S(2)}, u32[]{:S(2)}) collective-permute-start(bf16[32,16]{0,1:T(8,128)(2,1)S(1)} %pad_maximum_fusion.1), channel_id=1, source_target_pairs={{0,32},{16,48},{32,0},{48,16},{64,96},{80,112},{96,64},{112,80},{1... | collective-permute-start | bytes 3080 | tf_op jit(solution)/shard_map/ppermute | solution.py:328
  10.7 12.1 %collective-permute-start.3 = (bf16[64,16]{0,1:T(8,128)(2,1)S(1)}, bf16[64,16]{0,1:T(8,128)(2,1)S(1)}, u32[]{:S(2)}, u32[]{:S(2)}) collective-permute-start(bf16[64,16]{0,1:T(8,128)(2,1)S(1)} %pad_maximum_fusion.2), channel_id=1, source_target_pairs={{0,64},{16,80},{32,96},{48,112},{64,0},{80,16},{96,32},{112,48},{1... | collective-permute-start | bytes 6152 | tf_op jit(solution)/shard_map/ppermute | solution.py:328
  17.5 5.5 %copy-start.4 = (s32[128]{0:T(128)S(1)}, s32[128]{0:T(128)}, u32[]{:S(2)}) copy-start(s32[128]{0:T(128)} %pair.1) | copy-start | bytes 1540
  41.9 6.4 %copy-start.2 = (bf16[150,9600]{1,0:T(8,128)(2,1)S(1)}, bf16[150,9600]{1,0:T(8,128)(2,1)}, u32[]{:S(2)}) copy-start(bf16[150,9600]{1,0:T(8,128)(2,1)} %eri_ref.1) | copy-start | bytes 8640004
  41.9 6.4 %copy-start.3 = (s32[1200]{0:T(1024)S(1)}, s32[1200]{0:T(1024)}, u32[]{:S(2)}) copy-start(s32[1200]{0:T(1024)} %virt) | copy-start | bytes 14404

commit v4 on v3

--- a/solution.py
+++ b/solution.py
@@ -1,5 +1,3 @@
-import functools
-
 import jax
 import jax.numpy as jnp
 from jax import lax
@@ -66,6 +64,16 @@
     b_row = pltpu.roll(whole, TURN - b_at, 1)[0:1, 0:B_PAD]
     a_row = jnp.where(iota((1, A_PAD), 1) < A_ROWS, a_row, 64)
     return a_row, jnp.where(iota((1, B_PAD), 1) < B_COLS, b_row, 16)
+
+
+def own_irreps(b_row):
+    me = lax.axis_index("depth")
+    rank_row, _, _ = ranks(b_row)
+    beta = []
+    for i in range(PER):
+        mine = rank_row == i * LAYERS + me
+        beta.append(jnp.sum(jnp.where(mine, b_row, 0).astype(F32), axis=1, keepdims=True).astype(I32))
+    return beta
 
 
 def class_counts(labels):
@@ -151,7 +159,8 @@
     slot_row, _, p_col = slots(pair_ref)
     g_row = g_ref[0:1, META + CDS : META + 2 * CDS].astype(I32)
     for k in range(16):
-        block = (lax.axis_index("row") ^ (k & 1)) * 8 + (lax.axis_index("col") ^ (k >> 1))
+        apart = (k >> 1 & 1) * 4 + (k >> 2 & 1) + (k >> 3) * 2
+        block = (lax.axis_index("row") ^ (k & 1)) * 8 + (lax.axis_index("col") ^ apart)
         amps[pl.ds(pl.multiple_of(block * 8, 8), 8), :] = amp_ref[k * 8 : (k + 1) * 8, :].astype(F32)
     allowed = jnp.where(p_col == g_row, amps[...], 0.0).astype(BF)
     in_slot = ones(iota((CAP_IN, 128), 0) == slot_row).astype(BF)
@@ -171,11 +180,7 @@
         notes[CAP_IN : CAP_IN + 8, at] = tail[c * CAP_IN : c * CAP_IN + 8, META + CDS : META + 2 * CDS]
     over_ref[0] = jnp.max(notes[CAP_IN + 1 : CAP_IN + 2, :]).astype(I32)
     a_row, b_row = irreps(v_ref, turn)
-    rank_row, _, _ = ranks(b_row)
-    beta = []
-    for i in range(PER):
-        mine = rank_row == i * LAYERS + me
-        beta.append(jnp.sum(jnp.where(mine, b_row, 0).astype(F32), axis=1, keepdims=True).astype(I32))
+    beta = own_irreps(b_row)
 
     g_row = notes[CAP_IN : CAP_IN + 1, :].astype(I32)
     g_col = to_col(g_row)
@@ -209,10 +214,10 @@
                     keep, got[i * 64 : (i + 1) * 64, :], 0.0
                 ).astype(BF)
 
-    p_row = pair_ref[...]
     _, slot_col, p_col = slots(pair_ref)
     from_slot = ones(iota((128, CAP_IN), 1) == slot_col).astype(BF)
     allowed = jnp.where(p_col == g_row, dot(from_slot, notes[0:CAP_IN, :].astype(BF)), 0.0).astype(BF)
+    p_row = pair_ref[...]
     same2 = jnp.right_shift(iota(square, 0), 3) == jnp.right_shift(iota(square, 1), 3)
     earlier2 = jnp.logical_and(same2, iota(square, 0) < iota(square, 1))
     order2 = jnp.sum(ones(jnp.logical_and(earlier2, p_row == p_col)), axis=0, keepdims=True)
@@ -242,47 +247,63 @@
         pair_out[:, n : n + w] = stage[:, 0:w].astype(BF)
 
 
-def unpack_kernel(stride, gap, pair, v_ref, y_ref, o_ref, hot, both, sym, j_ref, turn):
-    step = pl.program_id(0)
+def unpack_tables(stride, gap, pair, v_ref, hot, sym, j_ref, turn):
     me = lax.axis_index("depth")
     labels = [pair[me * OWN_IJ + j] for j in range(OWN_IJ)]
     width = hot.shape[1]
-
-    @pl.when(step == 0)
-    def _():
-        a_row, b_row = irreps(v_ref, turn)
-        count, order = class_counts(labels)
-        for y in range(8):
-            j_ref[y] = count[y]
-        rank_row, rank_col, b_col = ranks(b_row)
-        same = jnp.logical_and((rank_row & 15) == (rank_col & 15), rank_row < rank_col)
-        diff = b_col ^ b_row
-        before = [jnp.sum(ones(jnp.logical_and(same, diff == y)), axis=1, keepdims=True) for y in range(8)]
-        first = (LAYERS - 1 - (rank_col & 15)) * stride
-        for j in range(OWN_IJ):
-            place = sum(j_ref[y ^ labels[j]].astype(F32) * before[y] for y in range(8)) + order[j].astype(F32)
-            place = first + place.astype(I32)
-            for t in range(2):
-                mine = place[t * HALF : (t + 1) * HALF, :]
-                lane = iota((HALF, width), 1)
-                at = (t * OWN_IJ + j) * HALF
-                hot[at : at + HALF, :] = ones(jnp.logical_or(lane == mine, lane == mine + gap)).astype(BF)
-        sym[...] = b_col ^ a_row
-        if y_ref.dtype == F32:
-            whole = y_ref[...]
-            top = whole.astype(BF)
-            both[0:gap, :] = top
-            both[gap : 2 * gap, :] = (whole - top.astype(F32)).astype(BF)
-
-    terms = both if y_ref.dtype == F32 else y_ref
+    a_row, b_row = irreps(v_ref, turn)
+    count, order = class_counts(labels)
+    for y in range(8):
+        j_ref[y] = count[y]
+    rank_row, rank_col, b_col = ranks(b_row)
+    same = jnp.logical_and((rank_row & 15) == (rank_col & 15), rank_row < rank_col)
+    diff = b_col ^ b_row
+    before = [jnp.sum(ones(jnp.logical_and(same, diff == y)), axis=1, keepdims=True) for y in range(8)]
+    first = (LAYERS - 1 - (rank_col & 15)) * stride
+    for j in range(OWN_IJ):
+        place = sum(j_ref[y ^ labels[j]].astype(F32) * before[y] for y in range(8)) + order[j].astype(F32)
+        place = first + place.astype(I32)
+        for t in range(2):
+            mine = place[t * HALF : (t + 1) * HALF, :]
+            lane = iota((HALF, width), 1)
+            at = (t * OWN_IJ + j) * HALF
+            hot[at : at + HALF, :] = ones(jnp.logical_or(lane == mine, lane == mine + gap)).astype(BF)
+    sym[...] = b_col ^ a_row
+
+
+def unpack_step(pair, hot, sym, terms, o_ref):
+    step = pl.program_id(0)
+    me = lax.axis_index("depth")
     rows = OWN_IJ * HALF
     of_step = hot[pl.ds(pl.multiple_of(step * rows, rows), rows), :]
     ab = sym[pl.ds(pl.multiple_of(step * HALF, HALF), HALF), :]
     for n, w, real in ((0, 256, 256), (256, 256, 256), (512, 128, A_ROWS - 512)):
         got = dot(of_step, terms[:, n : n + w])
         for j in range(OWN_IJ):
-            part = jnp.where(ab[:, n : n + w] == labels[j], got[j * HALF : (j + 1) * HALF, :], 0.0)
+            label = pair[me * OWN_IJ + j]
+            part = jnp.where(ab[:, n : n + w] == label, got[j * HALF : (j + 1) * HALF, :], 0.0)
             o_ref[:, j * A_ROWS + n : j * A_ROWS + n + real] = part[:, :real]
+
+
+def unpack_kernel(pair, hot, sym, y_ref, o_ref):
+    unpack_step(pair, hot, sym, y_ref, o_ref)
+
+
+def full_unpack_kernel(pair, v_ref, y_ref, o_ref, hot, both, sym, j_ref, turn):
+    @pl.when(pl.program_id(0) == 0)
+    def _():
+        gap = LAYERS * CAP_OUT
+        unpack_tables(CAP_OUT, gap, pair, v_ref, hot, sym, j_ref, turn)
+        whole = y_ref[...]
+        top = whole.astype(BF)
+        both[0:gap, :] = top
+        both[gap : 2 * gap, :] = (whole - top.astype(F32)).astype(BF)
+
+    unpack_step(pair, hot, sym, both, o_ref)
+
+
+def table_kernel(pair, v_ref, hot, sym, j_ref, turn):
+    unpack_tables(CAP_IN, CAP_LOW, pair, v_ref, hot, sym, j_ref, turn)
 
 
 VM = pl.BlockSpec(memory_space=pltpu.VMEM)
@@ -304,7 +325,8 @@
 def dense(rows, held, integrals, virt_irrep, pair_irrep):
     rows = rows.reshape(LAYERS, OWN_IJ, CDS)
     at = jnp.arange(LAYERS)
-    at = (lax.axis_index("row") ^ (at >> 3)) + 2 * (lax.axis_index("col") ^ (at & 7))
+    apart = lax.axis_index("col") ^ (at & 7)
+    at = (lax.axis_index("row") ^ (at >> 3)) + 2 * (apart >> 2) + 4 * (apart & 1) + 8 * (apart >> 1 & 1)
     amps = jnp.take(rows, at, axis=0).reshape(1, LAYERS * OWN_IJ, CDS)
     amps = jnp.broadcast_to(amps, (LAYERS, LAYERS * OWN_IJ, CDS))
     amps = lax.all_to_all(amps, "depth", 0, 0, tiled=True).transpose(1, 0, 2).reshape(-1, LAYERS * CDS)
@@ -333,27 +355,41 @@
     out_rows = LAYERS * CAP_OUT
     p_row = pair_irrep[None, :]
     turn = pltpu.VMEM((8, TURN), I32)
+    panel = jnp.concatenate([panel_c, panel_d])
     amps = jnp.concatenate([amplitudes, swap(amplitudes, "row", 2, 1)], axis=0)
-    amps, virt_irrep, panel_c, panel_d = lax.optimization_barrier((amps, virt_irrep, panel_c, panel_d))
-    near = swap(amps, "col", 8, 1)
+    amps, virt_irrep, panel = lax.optimization_barrier((amps, virt_irrep, panel))
+    far = swap(amps, "col", 8, 4)
     v_row = virt_irrep[None, :]
-    panel = jnp.concatenate([panel_c, panel_d])
-    near, v_row, panel = lax.optimization_barrier((near, v_row, panel))
-    amps = jnp.concatenate([amps, near], axis=0)
-    two = swap(amps, "col", 8, 2)
     place, notes = call(
         place_kernel,
         (virt_irrep, panel, pair_irrep, v_row, p_row),
         [SM, SM, SM, VM, VM],
         (jax.ShapeDtypeStruct((8, CDS * B_PAD), I32), jax.ShapeDtypeStruct((CAP_IN, 128), F32)),
         [pltpu.VMEM((8, B_PAD), F32), turn, pltpu.VMEM((8, 256), I32)],
-        4 * 10**8,
+        2 * 10**10,
         10**5,
         (VM, VM),
     )
-    two, place = lax.optimization_barrier((two, place))
-    amps = jnp.concatenate([amps, two], axis=0)
-    amps = jnp.concatenate([amps, swap(amps, "col", 8, 4)], axis=0)
+    far, place, notes = lax.optimization_barrier((far, place, notes))
+    amps = jnp.concatenate([amps, far], axis=0)
+    amps, v_row = lax.optimization_barrier((amps, v_row))
+    near = swap(amps, "col", 8, 1)
+    hot, sym = call(
+        table_kernel,
+        (pair_irrep, v_row),
+        [SM, VM],
+        (
+            jax.ShapeDtypeStruct((2 * OWN_IJ * HALF, rows), BF),
+            jax.ShapeDtypeStruct((B_PAD, A_PAD), I32),
+        ),
+        [pltpu.SMEM((8,), I32), turn],
+        10**9,
+        10**6,
+        (VM, VM),
+    )
+    near, hot, sym, place = lax.optimization_barrier((near, hot, sym, place))
+    amps = jnp.concatenate([amps, near], axis=0)
+    amps = jnp.concatenate([amps, swap(amps, "col", 8, 2)], axis=0)
     sent = call(
         pack_kernel,
         (notes, v_row, place, integrals),
@@ -411,43 +447,44 @@
 
     turned = [list(range(LAYERS - 1, -1, -1))]
 
-    def finish(array, stride, gap):
-        chunks = array.reshape(LAYERS, stride, A_PAD)
+    def finish(kernel, array, extra, specs, scratch):
+        chunks = array.reshape(LAYERS, -1, A_PAD)
         back = lax.all_to_all(chunks, "depth", 0, 0, tiled=True, axis_index_groups=turned)
-        back = back.reshape(array.shape)
-        width = 2 * gap if array.dtype == F32 else array.shape[0]
-        whole = lambda shape: pl.BlockSpec(shape, lambda t: (0, 0))
         return pl.pallas_call(
-            functools.partial(unpack_kernel, stride, gap),
+            kernel,
             out_shape=jax.ShapeDtypeStruct((B_COLS, OWN_IJ * A_ROWS), F32),
             grid=(2,),
-            in_specs=[SM, whole((1, NV)), whole(array.shape)],
+            in_specs=[SM, *specs, whole(array.shape)],
             out_specs=pl.BlockSpec((HALF, OWN_IJ * A_ROWS), lambda t: (t, 0)),
-            scratch_shapes=[
-                pltpu.VMEM((2 * OWN_IJ * HALF, width), BF),
-                pltpu.VMEM((width if array.dtype == F32 else 16, A_PAD), BF),
-                pltpu.VMEM((B_PAD, A_PAD), I32),
-                pltpu.SMEM((8,), I32),
-                turn,
-            ],
+            scratch_shapes=scratch,
             compiler_params=pltpu.CompilerParams(vmem_limit_bytes=VMEM_LIMIT),
             cost_estimate=pl.CostEstimate(
-                flops=4 * OWN_IJ * HALF * width * A_PAD,
+                flops=4 * OWN_IJ * HALF * rows * A_PAD,
                 bytes_accessed=4 * B_COLS * OWN_IJ * A_ROWS,
                 transcendentals=0,
             ),
-        )(pair_irrep, v_row, back)
-
-    def usual(part, terms, held, amps):
-        return finish(terms, CAP_IN, CAP_LOW)
-
-    def fuller(part, terms, held, amps):
-        return finish(part, CAP_OUT, out_rows)
-
-    def general(part, terms, held, amps):
+        )(pair_irrep, *extra, back.reshape(array.shape))
+
+    def whole(shape):
+        return pl.BlockSpec(shape, lambda t: (0, 0))
+
+    def usual(part, terms, held, amps, hot, sym):
+        return finish(unpack_kernel, terms, (hot, sym), [whole(hot.shape), whole(sym.shape)], [])
+
+    def fuller(part, terms, held, amps, hot, sym):
+        scratch = [
+            pltpu.VMEM((2 * OWN_IJ * HALF, 2 * out_rows), BF),
+            pltpu.VMEM((2 * out_rows, A_PAD), BF),
+            pltpu.VMEM((B_PAD, A_PAD), I32),
+            pltpu.SMEM((8,), I32),
+            turn,
+        ]
+        return finish(full_unpack_kernel, part, (v_row,), [whole((1, NV))], scratch)
+
+    def general(part, terms, held, amps, hot, sym):
         return dense(amps, held, integrals, virt_irrep, pair_irrep)
 
-    return lax.switch(over[0], (usual, fuller, general), part, terms, held, amps)
+    return lax.switch(over[0], (usual, fuller, general), part, terms, held, amps, hot, sym)
 
 
 def solution(mesh):

time: 68.2 us -> 65.8 us (0.965)
  starting transfers between devices: 12.1 us -> 9.84 us
  blocking collectives: 32.7 us -> 34.3 us
  Pallas kernels: 18.1 us -> 16.9 us
    ppermute x4, starting transfers between devices: 12.1 us -> 9.84 us  [swap(): return lax.ppermute(array, axis, [(d, d ^ step) for d in range(size)])]
    pallas_call x1, Pallas kernels: 5.08 us -> 3.58 us  [finish(): pl.pallas_call(kernel, out_shape=jax.ShapeDtypeStruct((B_COLS, OWN_IJ * A...]
    all_to_all x1, blocking collectives: 18.4 us -> 19.5 us  [body(): lax.all_to_all(sent.reshape(LAYERS, CAP_IN, A_PAD), 'depth', 0, 0, tiled=...]
    pallas_call x3 -> x4, Pallas kernels: 12.5 us -> 12.8 us  [call(): pl.pallas_call(kernel, out_shape=out, in_specs=specs, out_specs=outs, scr...]
  transfers between devices with their start and end apart: 4 -> 4, of which waited for: 2 -> 2; matrix products, arithmetic and copies ran while one was open for 2% -> 2% of each run, Pallas kernels for 10% -> 11%
where the time goes in v4:
time: 65.8 us; the launch traced here: 65.4 us
  blocking collectives  34.3 us (52%)
  Pallas kernels  16.9 us (26%)
  starting transfers between devices  9.84 us (15%)
  local copies, waits for them, and re-layouts  1.6 us (2%)
  other arithmetic  1.06 us (2%)
  waiting for transfers between devices  0.97 us (1%)
  between operations  0.71 us (1%)
    all_to_all x1, blocking collectives, body(): lax.all_to_all(sent.reshape(LAYERS, CAP_IN, A_PAD), 'depth', 0, 0, tiled=...  19.5 us
    all_to_all x1, blocking collectives, finish(): lax.all_to_all(chunks, 'depth', 0, 0, tiled=True, axis_index_groups=turned)  14.8 us
    pallas_call x4, Pallas kernels, call(): pl.pallas_call(kernel, out_shape=out, in_specs=specs, out_specs=outs, scr...  12.8 us
    ppermute x4, starting transfers between devices, swap(): return lax.ppermute(array, axis, [(d, d ^ step) for d in range(size)])  9.84 us
    pallas_call x1, Pallas kernels, finish(): pl.pallas_call(kernel, out_shape=jax.ShapeDtypeStruct((B_COLS, OWN_IJ * A...  3.58 us
  transfers between devices with their start and end apart: 4, of which 2 were waited for; matrix products, arithmetic and copies ran while one was open for 2% of the time, Pallas kernels for 11%

profile of v4, /device:TPU:2, one launch (start us, length us, event | category | flops | bytes accessed | tf_op | source)
XLA Modules:
  0.0 65.4 jit_solution(9190918812721017679)
XLA Ops:
  0.0 0.8 %copy.36 = bf16[8,16]{0,1:T(8,128)(2,1)S(1)} copy(bf16[8,16]{1,0:T(8,128)(2,1)} %param.9) | data formatting | bytes 512 | tf_op args[0]
  0.8 0.0 collective-permute-start
  0.8 0.7 %pad_add_fusion.panel = s32[32]{0:T(128)S(1)} fusion(s32[16]{0:T(128)} %param.14, s32[16]{0:T(128)} %param.13), kind=kLoop, calls=%fused_computation.24 | loop fusion | flops 32 | bytes 256 | tf_op jit(solution)/shard_map/concatenate | solution.py:358
  1.5 0.4 collective-permute-done
  1.9 0.1 pad_maximum_fusion
  2.0 7.2 %collective-permute-start.1 = (bf16[16,16]{0,1:T(8,128)(2,1)S(1)}, bf16[16,16]{0,1:T(8,128)(2,1)S(1)}, u32[]{:S(2)}, u32[]{:S(2)}) collective-permute-start(bf16[16,16]{0,1:T(8,128)(2,1)S(1)} %pad_maximum_fusion), channel_id=1, source_target_pairs={{0,64},{16,80},{32,96},{48,112},{64,0},{80,16},{96,32},{112,48},{1... | collective-permute-start | bytes 1544 | tf_op jit(solution)/shard_map/ppermute | solution.py:350
  9.2 0.7 %broadcast_in_dim.35.v_ref = s32[1,1200]{1,0:T(1,128)S(1)} reshape(s32[1200]{0:T(1024)} %virt) | data formatting | bytes 9600 | tf_op jit(solution)/shard_map/broadcast_in_dim | solution.py:362
  9.9 0.0 copy-start.5
  9.9 1.7 %shard_map.67 = (s32[8,2560]{1,0:T(8,128)S(1)}, f32[40,128]{1,0:T(8,128)S(1)}) custom-call(s32[1200]{0:T(1024)} %virt, s32[32]{0:T(128)S(1)} %pad_add_fusion.panel, s32[128]{0:T(128)} %pair.3, s32[1,1200]{1,0:T(1,128)S(1)} %broadcast_in_dim.35.v_ref, s32[1,128]{1,0:T(1,128)} %bitcast.49), custom_call_target="tpu_custom_call" | custom-call | flops 20000000000 | bytes 100000 | tf_op jit(solution)/shard_map/pallas_call | solution.py:314
  11.6 0.0 copy-start.2
  11.6 0.0 collective-permute-done.1
  11.6 0.1 pad_maximum_fusion.1
  11.7 1.0 %collective-permute-start.2 = (bf16[32,16]{0,1:T(8,128)(2,1)S(1)}, bf16[32,16]{0,1:T(8,128)(2,1)S(1)}, u32[]{:S(2)}, u32[]{:S(2)}) collective-permute-start(bf16[32,16]{0,1:T(8,128)(2,1)S(1)} %pad_maximum_fusion.1), channel_id=1, source_target_pairs={{0,16},{16,0},{32,48},{48,32},{64,80},{80,64},{96,112},{112,96},{1... | collective-permute-start | bytes 3080 | tf_op jit(solution)/shard_map/ppermute | solution.py:350
  12.7 0.0 copy-done.5
  12.7 2.0 %shard_map.68 = (bf16[1280,640]{1,0:T(8,128)(2,1)S(1)}, s32[160,640]{1,0:T(8,128)S(1)}) custom-call(s32[128]{0:T(128)S(1)} %copy-done.5, s32[1,1200]{1,0:T(1,128)S(1)} %broadcast_in_dim.35.v_ref), custom_call_target="tpu_custom_call" | custom-call | flops 1000000000 | bytes 1000000 | tf_op jit(solution)/shard_map/pallas_call | solution.py:314
  14.8 0.6 collective-permute-done.2
  15.3 0.1 pad_maximum_fusion.2
  15.4 1.6 %collective-permute-start.3 = (bf16[64,16]{0,1:T(8,128)(2,1)S(1)}, bf16[64,16]{0,1:T(8,128)(2,1)S(1)}, u32[]{:S(2)}, u32[]{:S(2)}) collective-permute-start(bf16[64,16]{0,1:T(8,128)(2,1)S(1)} %pad_maximum_fusion.2), channel_id=1, source_target_pairs={{0,32},{16,48},{32,0},{48,16},{64,96},{80,112},{96,64},{112,80},{1... | collective-permute-start | bytes 6152 | tf_op jit(solution)/shard_map/ppermute | solution.py:350
  17.0 0.0 copy-done.2
  17.0 3.4 %shard_map.69.x_in = bf16[640,640]{1,0:T(8,128)(2,1)S(1)} custom-call(f32[40,128]{1,0:T(8,128)S(1)} %get-tuple-element.71.g_ref, s32[1,1200]{1,0:T(1,128)S(1)} %broadcast_in_dim.35.v_ref, s32[8,2560]{1,0:T(8,128)S(1)} %get-tuple-element.77.q_ref, bf16[150,9600]{1,0:T(8,128)(2,1)S(1)} %copy-done.2), custom_call_target="tpu_custom_call" | custom-call | flops 2097152000 | bytes 2880000 | tf_op jit(solution)/shard_map/pallas_call | solution.py:314
  20.4 0.0 collective-permute-done.3
  20.4 0.1 pad_maximum_fusion.3
  20.5 0.1 copy.37.amp_ref
  20.6 0.5 shard_map.70
  21.1 19.5 %all_to_all.27 = bf16[16,40,640]{2,1,0:T(8,128)(2,1)S(1)} all-to-all(bf16[16,40,640]{2,1,0:T(8,128)(2,1)S(1)} %bitcast.42), channel_id=1, replica_groups=mesh['row'=2,'col'=8,'depth'=16] {'depth'}, dimensions={0} | all-to-all | bytes 1638400 | tf_op jit(solution)/shard_map/all_to_all | solution.py:423
  40.6 0.0 copy-start.3
  40.6 0.0 copy-start.4
  40.6 5.7 %shard_map.71 = (f32[384,640]{1,0:T(8,128)S(1)}, bf16[640,640]{1,0:T(8,128)(2,1)S(1)}, s32[1]{0:T(128)}) custom-call(s32[1,1200]{1,0:T(1,128)S(1)} %broadcast_in_dim.35.v_ref, s32[1,128]{1,0:T(1,128)S(1)} %bitcast.51, bf16[640,640]{1,0:T(8,128)(2,1)S(1)} %bitcast.45), custom_call_target="tpu_custom_call" | custom-call | flops 1782579200 | bytes 819200 | tf_op jit(solution)/shard_map/pallas_call | solution.py:314
  47.0 0.0 copy-done.3
  47.0 0.0 copy-done.4
  47.0 18.4 %conditional.1 = (f32[150,4800]{1,0:T(8,128)}) conditional(s32[]{:T(128)} %bitcast.17, (bf16[640,640]{1,0:T(8,128)(2,1)S(1)}, s32[128]{0:T(128)S(1)}, bf16[1280,640]{1,0:T(8,128)(2,1)S(1)}, s32[160,640]{1,0:T(8,128)S(1)}) %tuple.35, (f32[384,640]{1,0:T(8,128)S(1)}, s32[128]{0:T(128)S(1)}, s32[1,1200]{1,0:T(1,128)S(1)}) %tuple.36, ...), branch_computations={%region_0.0_spmd, %region_1.0_spmd, %region_2.3_spmd} | conditional | flops 1048576000 | bytes 107062904 | solution.py:487
  47.0 14.8 %all_to_all.25 = bf16[16,40,640]{2,1,0:T(8,128)(2,1)S(1)} all-to-all(bf16[16,40,640]{2,1,0:T(8,128)(2,1)S(1)} %bitcast.47), channel_id=1, replica_groups={{15,14,13,12,11,10,9,8,7,6,5,4,3,2,1,0},{31,30,29,28,27,26,25,24,23,22,..., dimensions={0} | all-to-all | bytes 1638400 | tf_op jit(solution)/shard_map/cond/branch_0_fun/all_to_all | solution.py:452
  61.8 3.6 %branch_0_fun.1 = f32[150,4800]{1,0:T(8,128)} custom-call(s32[128]{0:T(128)S(1)} %get-tuple-element.32.pair, bf16[1280,640]{1,0:T(8,128)(2,1)S(1)} %get-tuple-element.34.hot, s32[160,640]{1,0:T(8,128)S(1)} %get-tuple-element.35.sym, bf16[640,640]{1,0:T(8,128)(2,1)S(1)} %bitcast.43), custom_call_target="tpu_custom_call" | custom-call | flops 1048576000 | bytes 2880000 | tf_op jit(solution)/shard_map/cond/branch_0_fun/pallas_call | solution.py:453
Async XLA Ops:
  0.8 1.2 %collective-permute-start = (bf16[8,16]{0,1:T(8,128)(2,1)S(1)}, bf16[8,16]{0,1:T(8,128)(2,1)S(1)}, u32[]{:S(2)}, u32[]{:S(2)}) collective-permute-start(bf16[8,16]{0,1:T(8,128)(2,1)S(1)} %copy.36), channel_id=1, source_target_pairs={{0,128},{128,0},{1,129},{129,1},{2,130},{130,2},{3,131},{131,3},{4... | collective-permute-start | bytes 776 | tf_op jit(solution)/shard_map/ppermute | solution.py:350
  2.0 9.6 %collective-permute-start.1 = (bf16[16,16]{0,1:T(8,128)(2,1)S(1)}, bf16[16,16]{0,1:T(8,128)(2,1)S(1)}, u32[]{:S(2)}, u32[]{:S(2)}) collective-permute-start(bf16[16,16]{0,1:T(8,128)(2,1)S(1)} %pad_maximum_fusion), channel_id=1, source_target_pairs={{0,64},{16,80},{32,96},{48,112},{64,0},{80,16},{96,32},{112,48},{1... | collective-permute-start | bytes 1544 | tf_op jit(solution)/shard_map/ppermute | solution.py:350
  9.9 2.8 %copy-start.5 = (s32[128]{0:T(128)S(1)}, s32[128]{0:T(128)}, u32[]{:S(2)}) copy-start(s32[128]{0:T(128)} %pair.3) | copy-start | bytes 1540
  11.6 5.4 %copy-start.2 = (bf16[150,9600]{1,0:T(8,128)(2,1)S(1)}, bf16[150,9600]{1,0:T(8,128)(2,1)}, u32[]{:S(2)}) copy-start(bf16[150,9600]{1,0:T(8,128)(2,1)} %eri_ref.1) | copy-start | bytes 8640004
  11.7 3.6 %collective-permute-start.2 = (bf16[32,16]{0,1:T(8,128)(2,1)S(1)}, bf16[32,16]{0,1:T(8,128)(2,1)S(1)}, u32[]{:S(2)}, u32[]{:S(2)}) collective-permute-start(bf16[32,16]{0,1:T(8,128)(2,1)S(1)} %pad_maximum_fusion.1), channel_id=1, source_target_pairs={{0,16},{16,0},{32,48},{48,32},{64,80},{80,64},{96,112},{112,96},{1... | collective-permute-start | bytes 3080 | tf_op jit(solution)/shard_map/ppermute | solution.py:350
  15.4 5.0 %collective-permute-start.3 = (bf16[64,16]{0,1:T(8,128)(2,1)S(1)}, bf16[64,16]{0,1:T(8,128)(2,1)S(1)}, u32[]{:S(2)}, u32[]{:S(2)}) collective-permute-start(bf16[64,16]{0,1:T(8,128)(2,1)S(1)} %pad_maximum_fusion.2), channel_id=1, source_target_pairs={{0,32},{16,48},{32,0},{48,16},{64,96},{80,112},{96,64},{112,80},{1... | collective-permute-start | bytes 6152 | tf_op jit(solution)/shard_map/ppermute | solution.py:350
  40.6 6.4 %copy-start.3 = (bf16[150,9600]{1,0:T(8,128)(2,1)S(1)}, bf16[150,9600]{1,0:T(8,128)(2,1)}, u32[]{:S(2)}) copy-start(bf16[150,9600]{1,0:T(8,128)(2,1)} %eri_ref.1) | copy-start | bytes 8640004
  40.6 6.4 %copy-start.4 = (s32[1200]{0:T(1024)S(1)}, s32[1200]{0:T(1024)}, u32[]{:S(2)}) copy-start(s32[1200]{0:T(1024)} %virt) | copy-start | bytes 14404

commit v5 on v4

--- a/solution.py
+++ b/solution.py
@@ -54,10 +54,8 @@
     return rank_row, rank_col, jnp.right_shift(key_col, 8)
 
 
-def irreps(v_ref, turn):
-    turn[:, 0:NV] = jnp.broadcast_to(v_ref[...], (8, NV))
-    turn[:, NV:] = jnp.zeros((8, TURN - NV), I32)
-    whole = turn[...]
+def irreps(v_ref):
+    whole = jnp.broadcast_to(v_ref[...], (8, TURN))
     a_at = lax.axis_index("row") * A_ROWS
     b_at = lax.axis_index("col") * B_COLS
     a_row = pltpu.roll(whole, TURN - a_at, 1)[0:1, 0:A_PAD]
@@ -92,10 +90,10 @@
     return row.astype(I32), col.astype(I32), p_col
 
 
-def place_kernel(virt, panel, pair, v_ref, pair_ref, q_ref, m_ref, s_ref, turn, each):
+def place_kernel(labels, pair, v_ref, pair_ref, q_ref, m_ref, s_ref, each):
     me = lax.axis_index("depth")
-    _, b_row = irreps(v_ref, turn)
-    g = [virt[panel[j]] ^ virt[panel[CDS + j]] for j in range(CDS)]
+    _, b_row = irreps(v_ref)
+    g = [labels[0, labels[0, NV + j]] ^ labels[0, labels[0, NV + CDS + j]] for j in range(CDS)]
     rank_row, rank_col, b_col = ranks(b_row)
     same = jnp.logical_and((rank_row & 15) == (rank_col & 15), rank_col < rank_row)
     diff = b_col ^ b_row
@@ -111,7 +109,7 @@
 
     own = [pair[me * OWN_IJ + j] for j in range(OWN_IJ)]
     for c in range(8):
-        each[c : c + 1, 0:B_COLS] = turn[0:1, c * B_COLS : (c + 1) * B_COLS]
+        each[c : c + 1, 0:B_COLS] = v_ref[0:1, c * B_COLS : (c + 1) * B_COLS]
     of_col = each[:, 0:B_COLS]
     chunk = jnp.maximum(15 - iota((8, 128), 1), 0)
     start = jnp.zeros((8, 1), I32)
@@ -136,8 +134,8 @@
     m_ref[1:2, META + CDS : META + 2 * CDS] = jnp.broadcast_to(over, (1, CDS))
 
 
-def pack_kernel(g_ref, v_ref, q_ref, eri_ref, x_ref, hot, masked, turn):
-    a_row, b_row = irreps(v_ref, turn)
+def pack_kernel(g_ref, v_ref, q_ref, eri_ref, x_ref, hot, masked):
+    a_row, b_row = irreps(v_ref)
     b_col = to_col(b_row)
     rows = LAYERS * CAP_IN
     for t in range(CDS * B_PAD // 512):
@@ -171,7 +169,7 @@
     x_ref[...] = (x_in[...].astype(F32) + whole).astype(BF)
 
 
-def compute_kernel(v_ref, pair_ref, y_ref, x_ref, pair_out, over_ref, hot, eri, amp, hot2, turn, notes, tail, stage):
+def compute_kernel(v_ref, pair_ref, y_ref, x_ref, pair_out, over_ref, hot, eri, amp, hot2, notes, tail, stage):
     me = lax.axis_index("depth")
     tail[...] = y_ref[:, A_PAD - 128 : A_PAD].astype(F32)
     for c in range(LAYERS):
@@ -179,7 +177,7 @@
         notes[0:CAP_IN, at] = tail[c * CAP_IN : (c + 1) * CAP_IN, META : META + CDS]
         notes[CAP_IN : CAP_IN + 8, at] = tail[c * CAP_IN : c * CAP_IN + 8, META + CDS : META + 2 * CDS]
     over_ref[0] = jnp.max(notes[CAP_IN + 1 : CAP_IN + 2, :]).astype(I32)
-    a_row, b_row = irreps(v_ref, turn)
+    a_row, b_row = irreps(v_ref)
     beta = own_irreps(b_row)
 
     g_row = notes[CAP_IN : CAP_IN + 1, :].astype(I32)
@@ -247,11 +245,11 @@
         pair_out[:, n : n + w] = stage[:, 0:w].astype(BF)
 
 
-def unpack_tables(stride, gap, pair, v_ref, hot, sym, j_ref, turn):
+def unpack_tables(stride, gap, pair, v_ref, hot, sym, j_ref):
     me = lax.axis_index("depth")
     labels = [pair[me * OWN_IJ + j] for j in range(OWN_IJ)]
     width = hot.shape[1]
-    a_row, b_row = irreps(v_ref, turn)
+    a_row, b_row = irreps(v_ref)
     count, order = class_counts(labels)
     for y in range(8):
         j_ref[y] = count[y]
@@ -289,11 +287,11 @@
     unpack_step(pair, hot, sym, y_ref, o_ref)
 
 
-def full_unpack_kernel(pair, v_ref, y_ref, o_ref, hot, both, sym, j_ref, turn):
+def full_unpack_kernel(pair, v_ref, y_ref, o_ref, hot, both, sym, j_ref):
     @pl.when(pl.program_id(0) == 0)
     def _():
         gap = LAYERS * CAP_OUT
-        unpack_tables(CAP_OUT, gap, pair, v_ref, hot, sym, j_ref, turn)
+        unpack_tables(CAP_OUT, gap, pair, v_ref, hot, sym, j_ref)
         whole = y_ref[...]
         top = whole.astype(BF)
         both[0:gap, :] = top
@@ -302,8 +300,8 @@
     unpack_step(pair, hot, sym, both, o_ref)
 
 
-def table_kernel(pair, v_ref, hot, sym, j_ref, turn):
-    unpack_tables(CAP_IN, CAP_LOW, pair, v_ref, hot, sym, j_ref, turn)
+def table_kernel(pair, v_ref, hot, sym, j_ref):
+    unpack_tables(CAP_IN, CAP_LOW, pair, v_ref, hot, sym, j_ref)
 
 
 VM = pl.BlockSpec(memory_space=pltpu.VMEM)
@@ -354,18 +352,16 @@
     rows = LAYERS * CAP_IN
     out_rows = LAYERS * CAP_OUT
     p_row = pair_irrep[None, :]
-    turn = pltpu.VMEM((8, TURN), I32)
-    panel = jnp.concatenate([panel_c, panel_d])
+    v_row = jnp.concatenate([virt_irrep, panel_c, panel_d, jnp.zeros(TURN - NV - 2 * CDS, I32)])[None, :]
     amps = jnp.concatenate([amplitudes, swap(amplitudes, "row", 2, 1)], axis=0)
-    amps, virt_irrep, panel = lax.optimization_barrier((amps, virt_irrep, panel))
+    amps, v_row = lax.optimization_barrier((amps, v_row))
     far = swap(amps, "col", 8, 4)
-    v_row = virt_irrep[None, :]
     place, notes = call(
         place_kernel,
-        (virt_irrep, panel, pair_irrep, v_row, p_row),
-        [SM, SM, SM, VM, VM],
+        (v_row, pair_irrep, v_row, p_row),
+        [SM, SM, VM, VM],
         (jax.ShapeDtypeStruct((8, CDS * B_PAD), I32), jax.ShapeDtypeStruct((CAP_IN, 128), F32)),
-        [pltpu.VMEM((8, B_PAD), F32), turn, pltpu.VMEM((8, 256), I32)],
+        [pltpu.VMEM((8, B_PAD), F32), pltpu.VMEM((8, 256), I32)],
         2 * 10**10,
         10**5,
         (VM, VM),
@@ -382,7 +378,7 @@
             jax.ShapeDtypeStruct((2 * OWN_IJ * HALF, rows), BF),
             jax.ShapeDtypeStruct((B_PAD, A_PAD), I32),
         ),
-        [pltpu.SMEM((8,), I32), turn],
+        [pltpu.SMEM((8,), I32)],
         10**9,
         10**6,
         (VM, VM),
@@ -398,7 +394,6 @@
         [
             pltpu.VMEM((rows, CDS * B_PAD), BF),
             pltpu.VMEM((CDS * B_PAD, A_PAD), BF),
-            turn,
         ],
         2 * rows * CDS * B_PAD * A_PAD,
         2 * B_COLS * CDS * A_ROWS,
@@ -435,7 +430,6 @@
             pltpu.VMEM((PER * 256, A_PAD), BF),
             pltpu.VMEM((out_rows, PER * 256), BF),
             pltpu.VMEM((out_rows, 128), BF),
-            turn,
             pltpu.VMEM((CAP_IN + 8, LAYERS * CDS), F32),
             pltpu.VMEM((rows, 128), F32),
             pltpu.VMEM((rows, 256), F32),
@@ -477,9 +471,8 @@
             pltpu.VMEM((2 * out_rows, A_PAD), BF),
             pltpu.VMEM((B_PAD, A_PAD), I32),
             pltpu.SMEM((8,), I32),
-            turn,
         ]
-        return finish(full_unpack_kernel, part, (v_row,), [whole((1, NV))], scratch)
+        return finish(full_unpack_kernel, part, (v_row,), [whole((1, TURN))], scratch)
 
     def general(part, terms, held, amps, hot, sym):
         return dense(amps, held, integrals, virt_irrep, pair_irrep)

time: 65.8 us -> 65.5 us (level)
  starting transfers between devices: 9.84 us -> 10.6 us
  other arithmetic: 1.06 us -> 0.31 us
    concatenate x0 -> x1, local copies, waits for them, and re-layouts: none -> 0.77 us  [body(): jnp.concatenate([virt_irrep, panel_c, panel_d, jnp.zeros(TURN - NV - 2 *...]
    concatenate x1 -> x0, other arithmetic: 0.75 us -> none  [body(): panel = jnp.concatenate([panel_c, panel_d])]
    ppermute x4, starting transfers between devices: 9.84 us -> 10.6 us  [swap(): return lax.ppermute(array, axis, [(d, d ^ step) for d in range(size)])]
    broadcast_in_dim x1 -> x2, local copies, waits for them, and re-layouts: 0.7 us -> 0.01 us  [the longest x1 0.01 us: body(): jnp.concatenate([virt_irrep, panel_c, panel_d, jnp.zeros(TURN - NV - 2 *...]
  transfers between devices with their start and end apart: 4 -> 4, of which waited for: 2 -> 2; matrix products, arithmetic and copies ran while one was open for 2% -> 1% of each run, Pallas kernels for 11% -> 11%
where the time goes in v5:
time: 65.5 us; the launch traced here: 65.1 us
  blocking collectives  34 us (52%)
  Pallas kernels  16.8 us (26%)
  starting transfers between devices  10.6 us (16%)
  local copies, waits for them, and re-layouts  1.68 us (3%)
  waiting for transfers between devices  0.94 us (1%)
  between operations  0.71 us (1%)
    all_to_all x1, blocking collectives, body(): lax.all_to_all(sent.reshape(LAYERS, CAP_IN, A_PAD), 'depth', 0, 0, tiled=...  19.3 us
    all_to_all x1, blocking collectives, finish(): lax.all_to_all(chunks, 'depth', 0, 0, tiled=True, axis_index_groups=turned)  14.8 us
    pallas_call x4, Pallas kernels, call(): pl.pallas_call(kernel, out_shape=out, in_specs=specs, out_specs=outs, scr...  12.8 us
    ppermute x4, starting transfers between devices, swap(): return lax.ppermute(array, axis, [(d, d ^ step) for d in range(size)])  10.6 us
    pallas_call x1, Pallas kernels, finish(): pl.pallas_call(kernel, out_shape=jax.ShapeDtypeStruct((B_COLS, OWN_IJ * A...  3.58 us
  transfers between devices with their start and end apart: 4, of which 2 were waited for; matrix products, arithmetic and copies ran while one was open for 1% of the time, Pallas kernels for 11%

profile of v5, /device:TPU:2, one launch (start us, length us, event | category | flops | bytes accessed | tf_op | source)
XLA Modules:
  0.0 65.1 jit_solution(18052692505111430814)
XLA Ops:
  0.0 0.8 %copy.36 = bf16[8,16]{0,1:T(8,128)(2,1)S(1)} copy(bf16[8,16]{1,0:T(8,128)(2,1)} %param.9) | data formatting | bytes 512 | tf_op args[0]
  0.8 0.0 collective-permute-start
  0.8 0.8 %concatenate.17 = s32[1280]{0:T(1024)S(1)} concatenate(s32[1200]{0:T(1024)} %param.11, s32[16]{0:T(128)} %param.13, s32[16]{0:T(128)} %param.14, s32[48]{0:T(128)S(1)} %broadcast_in_dim.38), dimensions={0} | concatenate | bytes 10240 | tf_op jit(solution)/shard_map/concatenate | solution.py:355
  1.5 0.4 collective-permute-done
  1.9 0.1 pad_maximum_fusion
  2.0 7.2 %collective-permute-start.1 = (bf16[16,16]{0,1:T(8,128)(2,1)S(1)}, bf16[16,16]{0,1:T(8,128)(2,1)S(1)}, u32[]{:S(2)}, u32[]{:S(2)}) collective-permute-start(bf16[16,16]{0,1:T(8,128)(2,1)S(1)} %pad_maximum_fusion), channel_id=1, source_target_pairs={{0,64},{16,80},{32,96},{48,112},{64,0},{80,16},{96,32},{112,48},{1... | collective-permute-start | bytes 1544 | tf_op jit(solution)/shard_map/ppermute | solution.py:348
  9.2 0.0 copy-start.5
  9.2 1.7 %shard_map.67 = (s32[8,2560]{1,0:T(8,128)S(1)}, f32[40,128]{1,0:T(8,128)S(1)}) custom-call(s32[1,1280]{1,0:T(1,128)S(1)} %broadcast_in_dim.39.labels.v_ref, s32[128]{0:T(128)} %pair.3, s32[1,1280]{1,0:T(1,128)S(1)} %broadcast_in_dim.39.labels.v_ref, s32[1,128]{1,0:T(1,128)} %bitcast.49), custom_call_target="tpu_custom_call" | custom-call | flops 20000000000 | bytes 100000 | tf_op jit(solution)/shard_map/pallas_call | solution.py:312
  10.9 0.0 copy-start.2
  10.9 0.0 collective-permute-done.1
  10.9 0.1 pad_maximum_fusion.1
  11.0 1.0 %collective-permute-start.2 = (bf16[32,16]{0,1:T(8,128)(2,1)S(1)}, bf16[32,16]{0,1:T(8,128)(2,1)S(1)}, u32[]{:S(2)}, u32[]{:S(2)}) collective-permute-start(bf16[32,16]{0,1:T(8,128)(2,1)S(1)} %pad_maximum_fusion.1), channel_id=1, source_target_pairs={{0,16},{16,0},{32,48},{48,32},{64,80},{80,64},{96,112},{112,96},{1... | collective-permute-start | bytes 3080 | tf_op jit(solution)/shard_map/ppermute | solution.py:348
  12.0 0.0 copy-done.5
  12.0 2.0 %shard_map.68 = (bf16[1280,640]{1,0:T(8,128)(2,1)S(1)}, s32[160,640]{1,0:T(8,128)S(1)}) custom-call(s32[128]{0:T(128)S(1)} %copy-done.5, s32[1,1280]{1,0:T(1,128)S(1)} %broadcast_in_dim.39.labels.v_ref), custom_call_target="tpu_custom_call" | custom-call | flops 1000000000 | bytes 1000000 | tf_op jit(solution)/shard_map/pallas_call | solution.py:312
  14.1 0.6 collective-permute-done.2
  14.6 0.1 pad_maximum_fusion.2
  14.7 2.3 %collective-permute-start.3 = (bf16[64,16]{0,1:T(8,128)(2,1)S(1)}, bf16[64,16]{0,1:T(8,128)(2,1)S(1)}, u32[]{:S(2)}, u32[]{:S(2)}) collective-permute-start(bf16[64,16]{0,1:T(8,128)(2,1)S(1)} %pad_maximum_fusion.2), channel_id=1, source_target_pairs={{0,32},{16,48},{32,0},{48,16},{64,96},{80,112},{96,64},{112,80},{1... | collective-permute-start | bytes 6152 | tf_op jit(solution)/shard_map/ppermute | solution.py:348
  17.0 0.0 copy-done.2
  17.0 3.4 %shard_map.69.x_in = bf16[640,640]{1,0:T(8,128)(2,1)S(1)} custom-call(f32[40,128]{1,0:T(8,128)S(1)} %get-tuple-element.69.g_ref, s32[1,1280]{1,0:T(1,128)S(1)} %broadcast_in_dim.39.labels.v_ref, s32[8,2560]{1,0:T(8,128)S(1)} %get-tuple-element.75.q_ref, bf16[150,9600]{1,0:T(8,128)(2,1)S(1)} %copy-done.2), custom_call_target="tpu_custom_call" | custom-call | flops 2097152000 | bytes 2880000 | tf_op jit(solution)/shard_map/pallas_call | solution.py:312
  20.4 0.0 collective-permute-done.3
  20.4 0.1 pad_maximum_fusion.3
  20.5 0.1 copy.37.amp_ref
  20.6 0.5 shard_map.70
  21.1 19.3 %all_to_all.27 = bf16[16,40,640]{2,1,0:T(8,128)(2,1)S(1)} all-to-all(bf16[16,40,640]{2,1,0:T(8,128)(2,1)S(1)} %bitcast.42), channel_id=1, replica_groups=mesh['row'=2,'col'=8,'depth'=16] {'depth'}, dimensions={0} | all-to-all | bytes 1638400 | tf_op jit(solution)/shard_map/all_to_all | solution.py:418
  40.4 0.0 copy-start.3
  40.4 0.0 copy-start.4
  40.4 5.7 %shard_map.71 = (f32[384,640]{1,0:T(8,128)S(1)}, bf16[640,640]{1,0:T(8,128)(2,1)S(1)}, s32[1]{0:T(128)}) custom-call(s32[1,1280]{1,0:T(1,128)S(1)} %broadcast_in_dim.39.labels.v_ref, s32[1,128]{1,0:T(1,128)S(1)} %bitcast.51, bf16[640,640]{1,0:T(8,128)(2,1)S(1)} %bitcast.45), custom_call_target="tpu_custom_call" | custom-call | flops 1782579200 | bytes 819200 | tf_op jit(solution)/shard_map/pallas_call | solution.py:312
  46.7 0.0 copy-done.3
  46.7 0.0 copy-done.4
  46.7 18.3 %conditional.1 = (f32[150,4800]{1,0:T(8,128)}) conditional(s32[]{:T(128)} %bitcast.17, (bf16[640,640]{1,0:T(8,128)(2,1)S(1)}, s32[128]{0:T(128)S(1)}, bf16[1280,640]{1,0:T(8,128)(2,1)S(1)}, s32[160,640]{1,0:T(8,128)S(1)}) %tuple.35, (f32[384,640]{1,0:T(8,128)S(1)}, s32[128]{0:T(128)S(1)}, s32[1,1280]{1,0:T(1,128)S(1)}) %tuple.36, ...), branch_computations={%region_0.0_spmd, %region_1.0_spmd, %region_2.3_spmd} | conditional | flops 1048576000 | bytes 107062904 | solution.py:480
  46.7 14.8 %all_to_all.25 = bf16[16,40,640]{2,1,0:T(8,128)(2,1)S(1)} all-to-all(bf16[16,40,640]{2,1,0:T(8,128)(2,1)S(1)} %bitcast.47), channel_id=1, replica_groups={{15,14,13,12,11,10,9,8,7,6,5,4,3,2,1,0},{31,30,29,28,27,26,25,24,23,22,..., dimensions={0} | all-to-all | bytes 1638400 | tf_op jit(solution)/shard_map/cond/branch_0_fun/all_to_all | solution.py:446
  61.5 3.6 %branch_0_fun.1 = f32[150,4800]{1,0:T(8,128)} custom-call(s32[128]{0:T(128)S(1)} %get-tuple-element.32.pair, bf16[1280,640]{1,0:T(8,128)(2,1)S(1)} %get-tuple-element.34.hot, s32[160,640]{1,0:T(8,128)S(1)} %get-tuple-element.35.sym, bf16[640,640]{1,0:T(8,128)(2,1)S(1)} %bitcast.43), custom_call_target="tpu_custom_call" | custom-call | flops 1048576000 | bytes 2880000 | tf_op jit(solution)/shard_map/cond/branch_0_fun/pallas_call | solution.py:447
  (2 shorter events, 0.0 us)
Async XLA Ops:
  0.8 1.2 %collective-permute-start = (bf16[8,16]{0,1:T(8,128)(2,1)S(1)}, bf16[8,16]{0,1:T(8,128)(2,1)S(1)}, u32[]{:S(2)}, u32[]{:S(2)}) collective-permute-start(bf16[8,16]{0,1:T(8,128)(2,1)S(1)} %copy.36), channel_id=1, source_target_pairs={{0,128},{128,0},{1,129},{129,1},{2,130},{130,2},{3,131},{131,3},{4... | collective-permute-start | bytes 776 | tf_op jit(solution)/shard_map/ppermute | solution.py:348
  2.0 8.9 %collective-permute-start.1 = (bf16[16,16]{0,1:T(8,128)(2,1)S(1)}, bf16[16,16]{0,1:T(8,128)(2,1)S(1)}, u32[]{:S(2)}, u32[]{:S(2)}) collective-permute-start(bf16[16,16]{0,1:T(8,128)(2,1)S(1)} %pad_maximum_fusion), channel_id=1, source_target_pairs={{0,64},{16,80},{32,96},{48,112},{64,0},{80,16},{96,32},{112,48},{1... | collective-permute-start | bytes 1544 | tf_op jit(solution)/shard_map/ppermute | solution.py:348
  9.2 2.8 %copy-start.5 = (s32[128]{0:T(128)S(1)}, s32[128]{0:T(128)}, u32[]{:S(2)}) copy-start(s32[128]{0:T(128)} %pair.3) | copy-start | bytes 1540
  10.9 6.1 %copy-start.2 = (bf16[150,9600]{1,0:T(8,128)(2,1)S(1)}, bf16[150,9600]{1,0:T(8,128)(2,1)}, u32[]{:S(2)}) copy-start(bf16[150,9600]{1,0:T(8,128)(2,1)} %eri_ref.1) | copy-start | bytes 8640004
  11.0 3.6 %collective-permute-start.2 = (bf16[32,16]{0,1:T(8,128)(2,1)S(1)}, bf16[32,16]{0,1:T(8,128)(2,1)S(1)}, u32[]{:S(2)}, u32[]{:S(2)}) collective-permute-start(bf16[32,16]{0,1:T(8,128)(2,1)S(1)} %pad_maximum_fusion.1), channel_id=1, source_target_pairs={{0,16},{16,0},{32,48},{48,32},{64,80},{80,64},{96,112},{112,96},{1... | collective-permute-start | bytes 3080 | tf_op jit(solution)/shard_map/ppermute | solution.py:348
  14.7 5.7 %collective-permute-start.3 = (bf16[64,16]{0,1:T(8,128)(2,1)S(1)}, bf16[64,16]{0,1:T(8,128)(2,1)S(1)}, u32[]{:S(2)}, u32[]{:S(2)}) collective-permute-start(bf16[64,16]{0,1:T(8,128)(2,1)S(1)} %pad_maximum_fusion.2), channel_id=1, source_target_pairs={{0,32},{16,48},{32,0},{48,16},{64,96},{80,112},{96,64},{112,80},{1... | collective-permute-start | bytes 6152 | tf_op jit(solution)/shard_map/ppermute | solution.py:348
  40.4 6.4 %copy-start.3 = (bf16[150,9600]{1,0:T(8,128)(2,1)S(1)}, bf16[150,9600]{1,0:T(8,128)(2,1)}, u32[]{:S(2)}) copy-start(bf16[150,9600]{1,0:T(8,128)(2,1)} %eri_ref.1) | copy-start | bytes 8640004
  40.4 6.4 %copy-start.4 = (s32[1200]{0:T(1024)S(1)}, s32[1200]{0:T(1024)}, u32[]{:S(2)}) copy-start(s32[1200]{0:T(1024)} %param.11) | copy-start | bytes 14404

commit v6 on v5

--- a/solution.py
+++ b/solution.py
@@ -228,7 +228,7 @@
     short = (16, 128)
     by_part2 = ones(jnp.right_shift(iota(short, 1), 3) == iota(short, 0)).astype(BF)
     place2 = dot(by_part2, (seen2 * count2).astype(BF)) + order2
-    place2 = place2.astype(I32) + (LAYERS - 1 - jnp.right_shift(iota((1, 128), 1), 3)) * CAP_OUT
+    place2 = place2.astype(I32) + jnp.right_shift(iota((1, 128), 1), 3) * CAP_OUT
     out_rows = LAYERS * CAP_OUT
     for i in range(PER):
         hot2[...] = ones(iota((out_rows, 128), 0) == place2[i : i + 1, :]).astype(BF)
@@ -257,7 +257,7 @@
     same = jnp.logical_and((rank_row & 15) == (rank_col & 15), rank_row < rank_col)
     diff = b_col ^ b_row
     before = [jnp.sum(ones(jnp.logical_and(same, diff == y)), axis=1, keepdims=True) for y in range(8)]
-    first = (LAYERS - 1 - (rank_col & 15)) * stride
+    first = (rank_col & 15) * stride
     for j in range(OWN_IJ):
         place = sum(j_ref[y ^ labels[j]].astype(F32) * before[y] for y in range(8)) + order[j].astype(F32)
         place = first + place.astype(I32)
@@ -439,11 +439,10 @@
         (VM, VM, SM),
     )
 
-    turned = [list(range(LAYERS - 1, -1, -1))]
 
     def finish(kernel, array, extra, specs, scratch):
         chunks = array.reshape(LAYERS, -1, A_PAD)
-        back = lax.all_to_all(chunks, "depth", 0, 0, tiled=True, axis_index_groups=turned)
+        back = lax.all_to_all(chunks, "depth", 0, 0, tiled=True)
         return pl.pallas_call(
             kernel,
             out_shape=jax.ShapeDtypeStruct((B_COLS, OWN_IJ * A_ROWS), F32),

time: 65.5 us -> 65.8 us (level)
  no operation moved by 1% of the time
where the time goes in v6:
time: 65.8 us; the launch traced here: 65.6 us
  blocking collectives  34.5 us (52%)
  Pallas kernels  16.9 us (26%)
  starting transfers between devices  10.6 us (16%)
  local copies, waits for them, and re-layouts  1.68 us (3%)
  waiting for transfers between devices  0.92 us (1%)
  between operations  0.71 us (1%)
    all_to_all x1, blocking collectives, body(): lax.all_to_all(sent.reshape(LAYERS, CAP_IN, A_PAD), 'depth', 0, 0, tiled=...  19.3 us
    all_to_all x1, blocking collectives, finish(): back = lax.all_to_all(chunks, 'depth', 0, 0, tiled=True)  15.2 us
    pallas_call x4, Pallas kernels, call(): pl.pallas_call(kernel, out_shape=out, in_specs=specs, out_specs=outs, scr...  12.8 us
    ppermute x4, starting transfers between devices, swap(): return lax.ppermute(array, axis, [(d, d ^ step) for d in range(size)])  10.6 us
    pallas_call x1, Pallas kernels, finish(): pl.pallas_call(kernel, out_shape=jax.ShapeDtypeStruct((B_COLS, OWN_IJ * A...  3.58 us
  transfers between devices with their start and end apart: 4, of which 2 were waited for; matrix products, arithmetic and copies ran while one was open for 1% of the time, Pallas kernels for 11%

profile of v6, /device:TPU:2, one launch (start us, length us, event | category | flops | bytes accessed | tf_op | source)
XLA Modules:
  0.0 65.6 jit_solution(6464951563797637183)
XLA Ops:
  0.0 0.8 %copy.36 = bf16[8,16]{0,1:T(8,128)(2,1)S(1)} copy(bf16[8,16]{1,0:T(8,128)(2,1)} %param.9) | data formatting | bytes 512 | tf_op args[0]
  0.8 0.0 collective-permute-start
  0.8 0.8 %concatenate.17 = s32[1280]{0:T(1024)S(1)} concatenate(s32[1200]{0:T(1024)} %param.11, s32[16]{0:T(128)} %param.13, s32[16]{0:T(128)} %param.14, s32[48]{0:T(128)S(1)} %broadcast_in_dim.38), dimensions={0} | concatenate | bytes 10240 | tf_op jit(solution)/shard_map/concatenate | solution.py:355
  1.5 0.4 collective-permute-done
  1.9 0.1 pad_maximum_fusion
  2.0 7.2 %collective-permute-start.1 = (bf16[16,16]{0,1:T(8,128)(2,1)S(1)}, bf16[16,16]{0,1:T(8,128)(2,1)S(1)}, u32[]{:S(2)}, u32[]{:S(2)}) collective-permute-start(bf16[16,16]{0,1:T(8,128)(2,1)S(1)} %pad_maximum_fusion), channel_id=1, source_target_pairs={{0,64},{16,80},{32,96},{48,112},{64,0},{80,16},{96,32},{112,48},{1... | collective-permute-start | bytes 1544 | tf_op jit(solution)/shard_map/ppermute | solution.py:348
  9.2 0.0 copy-start.5
  9.2 1.7 %shard_map.67 = (s32[8,2560]{1,0:T(8,128)S(1)}, f32[40,128]{1,0:T(8,128)S(1)}) custom-call(s32[1,1280]{1,0:T(1,128)S(1)} %broadcast_in_dim.39.labels.v_ref, s32[128]{0:T(128)} %pair.3, s32[1,1280]{1,0:T(1,128)S(1)} %broadcast_in_dim.39.labels.v_ref, s32[1,128]{1,0:T(1,128)} %bitcast.49), custom_call_target="tpu_custom_call" | custom-call | flops 20000000000 | bytes 100000 | tf_op jit(solution)/shard_map/pallas_call | solution.py:312
  10.9 0.0 copy-start.2
  10.9 0.0 collective-permute-done.1
  10.9 0.1 pad_maximum_fusion.1
  11.0 1.0 %collective-permute-start.2 = (bf16[32,16]{0,1:T(8,128)(2,1)S(1)}, bf16[32,16]{0,1:T(8,128)(2,1)S(1)}, u32[]{:S(2)}, u32[]{:S(2)}) collective-permute-start(bf16[32,16]{0,1:T(8,128)(2,1)S(1)} %pad_maximum_fusion.1), channel_id=1, source_target_pairs={{0,16},{16,0},{32,48},{48,32},{64,80},{80,64},{96,112},{112,96},{1... | collective-permute-start | bytes 3080 | tf_op jit(solution)/shard_map/ppermute | solution.py:348
  12.0 0.0 copy-done.5
  12.0 2.0 %shard_map.68 = (bf16[1280,640]{1,0:T(8,128)(2,1)S(1)}, s32[160,640]{1,0:T(8,128)S(1)}) custom-call(s32[128]{0:T(128)S(1)} %copy-done.5, s32[1,1280]{1,0:T(1,128)S(1)} %broadcast_in_dim.39.labels.v_ref), custom_call_target="tpu_custom_call" | custom-call | flops 1000000000 | bytes 1000000 | tf_op jit(solution)/shard_map/pallas_call | solution.py:312
  14.1 0.5 collective-permute-done.2
  14.6 0.1 pad_maximum_fusion.2
  14.7 2.3 %collective-permute-start.3 = (bf16[64,16]{0,1:T(8,128)(2,1)S(1)}, bf16[64,16]{0,1:T(8,128)(2,1)S(1)}, u32[]{:S(2)}, u32[]{:S(2)}) collective-permute-start(bf16[64,16]{0,1:T(8,128)(2,1)S(1)} %pad_maximum_fusion.2), channel_id=1, source_target_pairs={{0,32},{16,48},{32,0},{48,16},{64,96},{80,112},{96,64},{112,80},{1... | collective-permute-start | bytes 6152 | tf_op jit(solution)/shard_map/ppermute | solution.py:348
  17.0 0.0 copy-done.2
  17.0 3.4 %shard_map.69.x_in = bf16[640,640]{1,0:T(8,128)(2,1)S(1)} custom-call(f32[40,128]{1,0:T(8,128)S(1)} %get-tuple-element.69.g_ref, s32[1,1280]{1,0:T(1,128)S(1)} %broadcast_in_dim.39.labels.v_ref, s32[8,2560]{1,0:T(8,128)S(1)} %get-tuple-element.75.q_ref, bf16[150,9600]{1,0:T(8,128)(2,1)S(1)} %copy-done.2), custom_call_target="tpu_custom_call" | custom-call | flops 2097152000 | bytes 2880000 | tf_op jit(solution)/shard_map/pallas_call | solution.py:312
  20.4 0.0 collective-permute-done.3
  20.4 0.1 pad_maximum_fusion.3
  20.5 0.1 copy.37.amp_ref
  20.6 0.5 shard_map.70
  21.1 19.3 %all_to_all.27 = bf16[16,40,640]{2,1,0:T(8,128)(2,1)S(1)} all-to-all(bf16[16,40,640]{2,1,0:T(8,128)(2,1)S(1)} %bitcast.42), channel_id=1, replica_groups=mesh['row'=2,'col'=8,'depth'=16] {'depth'}, dimensions={0} | all-to-all | bytes 1638400 | tf_op jit(solution)/shard_map/all_to_all | solution.py:418
  40.4 0.0 copy-start.3
  40.4 0.0 copy-start.4
  40.4 5.7 %shard_map.71 = (f32[384,640]{1,0:T(8,128)S(1)}, bf16[640,640]{1,0:T(8,128)(2,1)S(1)}, s32[1]{0:T(128)}) custom-call(s32[1,1280]{1,0:T(1,128)S(1)} %broadcast_in_dim.39.labels.v_ref, s32[1,128]{1,0:T(1,128)S(1)} %bitcast.51, bf16[640,640]{1,0:T(8,128)(2,1)S(1)} %bitcast.45), custom_call_target="tpu_custom_call" | custom-call | flops 1782579200 | bytes 819200 | tf_op jit(solution)/shard_map/pallas_call | solution.py:312
  46.7 0.0 copy-done.3
  46.7 0.0 copy-done.4
  46.8 18.8 %conditional.1 = (f32[150,4800]{1,0:T(8,128)}) conditional(s32[]{:T(128)} %bitcast.17, (bf16[640,640]{1,0:T(8,128)(2,1)S(1)}, s32[128]{0:T(128)S(1)}, bf16[1280,640]{1,0:T(8,128)(2,1)S(1)}, s32[160,640]{1,0:T(8,128)S(1)}) %tuple.35, (f32[384,640]{1,0:T(8,128)S(1)}, s32[128]{0:T(128)S(1)}, s32[1,1280]{1,0:T(1,128)S(1)}) %tuple.36, ...), branch_computations={%region_0.0_spmd, %region_1.0_spmd, %region_2.3_spmd} | conditional | flops 1048576000 | bytes 107062904 | solution.py:479
  46.8 15.2 %all_to_all.25 = bf16[16,40,640]{2,1,0:T(8,128)(2,1)S(1)} all-to-all(bf16[16,40,640]{2,1,0:T(8,128)(2,1)S(1)} %bitcast.47), channel_id=1, replica_groups=mesh['row'=2,'col'=8,'depth'=16] {'depth'}, dimensions={0} | all-to-all | bytes 1638400 | tf_op jit(solution)/shard_map/cond/branch_0_fun/all_to_all | solution.py:445
  62.0 3.6 %branch_0_fun.1 = f32[150,4800]{1,0:T(8,128)} custom-call(s32[128]{0:T(128)S(1)} %get-tuple-element.32.pair, bf16[1280,640]{1,0:T(8,128)(2,1)S(1)} %get-tuple-element.34.hot, s32[160,640]{1,0:T(8,128)S(1)} %get-tuple-element.35.sym, bf16[640,640]{1,0:T(8,128)(2,1)S(1)} %bitcast.43), custom_call_target="tpu_custom_call" | custom-call | flops 1048576000 | bytes 2880000 | tf_op jit(solution)/shard_map/cond/branch_0_fun/pallas_call | solution.py:446
  (2 shorter events, 0.0 us)
Async XLA Ops:
  0.8 1.2 %collective-permute-start = (bf16[8,16]{0,1:T(8,128)(2,1)S(1)}, bf16[8,16]{0,1:T(8,128)(2,1)S(1)}, u32[]{:S(2)}, u32[]{:S(2)}) collective-permute-start(bf16[8,16]{0,1:T(8,128)(2,1)S(1)} %copy.36), channel_id=1, source_target_pairs={{0,128},{128,0},{1,129},{129,1},{2,130},{130,2},{3,131},{131,3},{4... | collective-permute-start | bytes 776 | tf_op jit(solution)/shard_map/ppermute | solution.py:348
  2.0 8.9 %collective-permute-start.1 = (bf16[16,16]{0,1:T(8,128)(2,1)S(1)}, bf16[16,16]{0,1:T(8,128)(2,1)S(1)}, u32[]{:S(2)}, u32[]{:S(2)}) collective-permute-start(bf16[16,16]{0,1:T(8,128)(2,1)S(1)} %pad_maximum_fusion), channel_id=1, source_target_pairs={{0,64},{16,80},{32,96},{48,112},{64,0},{80,16},{96,32},{112,48},{1... | collective-permute-start | bytes 1544 | tf_op jit(solution)/shard_map/ppermute | solution.py:348
  9.2 2.8 %copy-start.5 = (s32[128]{0:T(128)S(1)}, s32[128]{0:T(128)}, u32[]{:S(2)}) copy-start(s32[128]{0:T(128)} %pair.3) | copy-start | bytes 1540
  10.9 6.1 %copy-start.2 = (bf16[150,9600]{1,0:T(8,128)(2,1)S(1)}, bf16[150,9600]{1,0:T(8,128)(2,1)}, u32[]{:S(2)}) copy-start(bf16[150,9600]{1,0:T(8,128)(2,1)} %eri_ref.1) | copy-start | bytes 8640004
  11.0 3.6 %collective-permute-start.2 = (bf16[32,16]{0,1:T(8,128)(2,1)S(1)}, bf16[32,16]{0,1:T(8,128)(2,1)S(1)}, u32[]{:S(2)}, u32[]{:S(2)}) collective-permute-start(bf16[32,16]{0,1:T(8,128)(2,1)S(1)} %pad_maximum_fusion.1), channel_id=1, source_target_pairs={{0,16},{16,0},{32,48},{48,32},{64,80},{80,64},{96,112},{112,96},{1... | collective-permute-start | bytes 3080 | tf_op jit(solution)/shard_map/ppermute | solution.py:348
  14.7 5.7 %collective-permute-start.3 = (bf16[64,16]{0,1:T(8,128)(2,1)S(1)}, bf16[64,16]{0,1:T(8,128)(2,1)S(1)}, u32[]{:S(2)}, u32[]{:S(2)}) collective-permute-start(bf16[64,16]{0,1:T(8,128)(2,1)S(1)} %pad_maximum_fusion.2), channel_id=1, source_target_pairs={{0,32},{16,48},{32,0},{48,16},{64,96},{80,112},{96,64},{112,80},{1... | collective-permute-start | bytes 6152 | tf_op jit(solution)/shard_map/ppermute | solution.py:348
  40.4 6.4 %copy-start.3 = (bf16[150,9600]{1,0:T(8,128)(2,1)S(1)}, bf16[150,9600]{1,0:T(8,128)(2,1)}, u32[]{:S(2)}) copy-start(bf16[150,9600]{1,0:T(8,128)(2,1)} %eri_ref.1) | copy-start | bytes 8640004
  40.4 6.4 %copy-start.4 = (s32[1200]{0:T(1024)S(1)}, s32[1200]{0:T(1024)}, u32[]{:S(2)}) copy-start(s32[1200]{0:T(1024)} %param.11) | copy-start | bytes 14404
